TPU v7x, 32 devices: a whole 2x2x4 slice. The times are simulated.
32 devices in a mesh: wide: 4 (over z), pair: 4 (over y, x), chip: 2 (over core).
Axes of the slice: x: 2, y: 2, z: 4, core: 2. Of those that a mesh axis runs over, the one named last changes fastest.
Arguments:
- expression: bfloat16 [8192, 7000], P(('wide', 'pair', 'chip')), may hold values from 0 to 6, as said below
- noise: float32 [8192, 100], P(('wide', 'pair', 'chip')), may hold values from -6 to 6
- study: int32 [8192], P(('wide', 'pair', 'chip')), may hold values from 0 to 7
- measured_gene_mask: int32 [8, 7000], replicated, may hold values 0 or 1
- encoder_input_weight: bfloat16 [7000, 800], P(('pair', 'chip'), 'wide'), may hold values from -0.0625 to 0.0625
- enc_mid: bfloat16 [800, 800], P(('pair', 'chip'), 'wide'), may hold values from -0.21875 to 0.21875
- heads: bfloat16 [200, 800], P(('pair', 'chip'), 'wide'), may hold values from -0.21875 to 0.21875
- dec_in: bfloat16 [100, 800], P(None, 'wide'), may hold values from -0.625 to 0.625
- dec_mid: bfloat16 [800, 800], P(('pair', 'chip'), 'wide'), may hold values from -0.21875 to 0.21875
- dec_out: bfloat16 [7000, 800], P(('pair', 'chip'), 'wide'), may hold values from -0.21875 to 0.21875
- norm_params: bfloat16 [8, 800], P(('pair', 'chip'), 'wide'), may hold values from 0.5 to 1.5
- head_bias: float32 [200], replicated, may hold values from -3 to 3
- out_bias: float32 [7000], replicated, may hold values from -3 to 3
- running_stats: float32 [8, 800], P(('pair', 'chip'), 'wide'), may hold values from 0.5 to 1.5
Outputs:
- loss: float32 [], replicated
- input_grad: float32 [8192, 7000], P(('wide', 'pair', 'chip'))
- enc_in_grad: float32 [7000, 800], P(('pair', 'chip'), 'wide')
- enc_mid_grad: float32 [800, 800], P(('pair', 'chip'), 'wide')
- heads_grad: float32 [200, 800], P(('pair', 'chip'), 'wide')
- dec_in_grad: float32 [100, 800], P(None, 'wide')
- dec_mid_grad: float32 [800, 800], P(('pair', 'chip'), 'wide')
- dec_out_grad: float32 [7000, 800], P(('pair', 'chip'), 'wide')
- norm_grad: float32 [8, 800], P(('pair', 'chip'), 'wide')
- head_bias_grad: float32 [200], replicated
- out_bias_grad: float32 [7000], replicated
- running_next: float32 [8, 800], P(('pair', 'chip'), 'wide')
Inputs may be any that keep to these rules, and one draw needn't show every extreme that they name: Non-negative expression values.
All inputs are finite; a program needn't handle non-finite values.
Results may differ from a plain program's by a relative error of at most 0.014.
Values may be sent and summed in bfloat16 or wider, within the bound.
No kernel may reach another device: no remote copies, remote signals or barrier semaphores. Data moves between devices by JAX's collectives and lax.ppermute only.
A program may use at most 448 MiB of HBM per device.

v0:
```python
import jax
import jax.numpy as jnp
from jax import lax
from jax.sharding import PartitionSpec as P

ALPHA = 0.005
EPSILON = 1e-05
MOMENTUM = 0.1


def contract_rows(left, right):
    return lax.dot_general(
        left, right, (((0,), (0,)), ((), ())), preferred_element_type=jnp.float32
    )


def contract_cols(left, right):
    return lax.dot_general(
        left, right, (((1,), (1,)), ((), ())), preferred_element_type=jnp.float32
    )


def to_blocks(grad, row_parts, col_parts):
    rows, cols = grad.shape
    shaped = grad.reshape(row_parts, rows // row_parts, col_parts, cols // col_parts)
    return shaped.transpose(2, 0, 1, 3).reshape(
        col_parts * row_parts, rows // row_parts * (cols // col_parts)
    )


def batch_moments(pre_act, count_all):
    centre = lax.psum(jnp.sum(pre_act, axis=0), ("wide", "pair", "chip")) / count_all
    variance = (
        lax.psum(jnp.sum(jnp.square(pre_act - centre), axis=0), ("wide", "pair", "chip"))
        / count_all
    )
    return (centre, variance)


def normalize(pre_act, gain, shift, count_all):
    centre, variance = batch_moments(pre_act, count_all)
    inverse = lax.rsqrt(variance + EPSILON)
    scaled = (pre_act - centre) * inverse
    normed = scaled * gain + shift
    return (normed, scaled, inverse, centre, variance)


def norm_backward(upstream, normed, scaled, inverse, gain, count_all):
    gate_value = jax.nn.sigmoid(normed)
    back_normed = upstream * gate_value * (1.0 + normed * (1.0 - gate_value))
    shift_sum, gain_sum = lax.psum(
        (jnp.sum(back_normed, axis=0), jnp.sum(back_normed * scaled, axis=0)),
        ("wide", "pair", "chip"),
    )
    back_pre = (
        gain * inverse * (back_normed - shift_sum / count_all - scaled * gain_sum / count_all)
    )
    return (back_pre.astype(jnp.bfloat16), gain_sum, shift_sum)


def on_device(
    expression,
    noise,
    study,
    measured_gene_mask,
    encoder_input_weight,
    enc_mid,
    heads,
    dec_in,
    dec_mid,
    dec_out,
    norm_params,
    head_bias,
    out_bias,
    running_stats,
):
    count_all = expression.shape[0] * lax.axis_size(("wide", "pair", "chip"))
    latent = dec_in.shape[0]
    row_parts = (
        lax.all_gather(encoder_input_weight, ("pair", "chip"), axis=0, tiled=True),
        lax.all_gather(enc_mid, ("pair", "chip"), axis=0, tiled=True),
        lax.all_gather(heads, ("pair", "chip"), axis=0, tiled=True),
        lax.all_gather(dec_mid, ("pair", "chip"), axis=0, tiled=True),
        lax.all_gather(dec_out, ("pair", "chip"), axis=0, tiled=True),
        lax.all_gather(norm_params, ("pair", "chip"), axis=0, tiled=True),
    )
    gathered = (
        lax.all_gather(row_parts[0], "wide", axis=1, tiled=True),
        lax.all_gather(row_parts[1], "wide", axis=1, tiled=True),
        lax.all_gather(row_parts[2], "wide", axis=1, tiled=True),
        lax.all_gather(dec_in, "wide", axis=1, tiled=True),
        lax.all_gather(row_parts[3], "wide", axis=1, tiled=True),
        lax.all_gather(row_parts[4], "wide", axis=1, tiled=True),
        lax.all_gather(row_parts[5], "wide", axis=1, tiled=True),
    )
    w_enc_in, w_enc_mid, w_heads, w_dec_in, w_dec_mid, w_dec_out, norm_full = gathered
    gain_rows = norm_full[:4].astype(jnp.float32)
    shift_rows = norm_full[4:].astype(jnp.float32)
    study_labels = measured_gene_mask.shape[0]
    study_indicator = (study[:, None] == jnp.arange(study_labels, dtype=jnp.int32)[None, :]).astype(
        jnp.bfloat16
    )
    keep = jnp.dot(
        study_indicator, measured_gene_mask.astype(jnp.bfloat16), preferred_element_type=jnp.float32
    )
    pre_one = jnp.dot(expression, w_enc_in, preferred_element_type=jnp.float32)
    normed_one, scaled_one, inverse_one, centre_one, spread_one = normalize(
        pre_one, gain_rows[0], shift_rows[0], count_all
    )
    hidden_one = jax.nn.silu(normed_one).astype(jnp.bfloat16)
    pre_two = jnp.dot(hidden_one, w_enc_mid, preferred_element_type=jnp.float32)
    normed_two, scaled_two, inverse_two, centre_two, spread_two = normalize(
        pre_two, gain_rows[1], shift_rows[1], count_all
    )
    hidden_two = jax.nn.silu(normed_two).astype(jnp.bfloat16)
    encoded = contract_cols(hidden_two, w_heads) + head_bias
    latent_mean = encoded[:, :latent]
    logvar = encoded[:, latent:]
    spread_factor = jnp.exp(0.5 * logvar)
    code = (latent_mean + spread_factor * noise).astype(jnp.bfloat16)
    pre_three = jnp.dot(code, w_dec_in, preferred_element_type=jnp.float32)
    normed_three, scaled_three, inverse_three, centre_three, spread_three = normalize(
        pre_three, gain_rows[2], shift_rows[2], count_all
    )
    hidden_three = jax.nn.silu(normed_three).astype(jnp.bfloat16)
    pre_four = jnp.dot(hidden_three, w_dec_mid, preferred_element_type=jnp.float32)
    normed_four, scaled_four, inverse_four, centre_four, spread_four = normalize(
        pre_four, gain_rows[3], shift_rows[3], count_all
    )
    hidden_four = jax.nn.silu(normed_four).astype(jnp.bfloat16)
    out_pre = contract_cols(hidden_four, w_dec_out) + out_bias
    recon = jax.nn.softplus(out_pre)
    diff = recon - expression.astype(jnp.float32)
    recon_term = 0.5 * jnp.sum(keep * diff * diff, axis=1)
    exp_logvar = jnp.exp(logvar)
    kl_term = 0.5 * jnp.sum(exp_logvar + latent_mean * latent_mean - 1.0 - logvar, axis=1)
    loss_local = jnp.sum(recon_term + ALPHA * kl_term)
    row_again = (
        lax.all_gather(encoder_input_weight, ("pair", "chip"), axis=0, tiled=True),
        lax.all_gather(enc_mid, ("pair", "chip"), axis=0, tiled=True),
        lax.all_gather(heads, ("pair", "chip"), axis=0, tiled=True),
        lax.all_gather(dec_mid, ("pair", "chip"), axis=0, tiled=True),
        lax.all_gather(dec_out, ("pair", "chip"), axis=0, tiled=True),
    )
    back_full = (
        lax.all_gather(row_again[0], "wide", axis=1, tiled=True),
        lax.all_gather(row_again[1], "wide", axis=1, tiled=True),
        lax.all_gather(row_again[2], "wide", axis=1, tiled=True),
        lax.all_gather(dec_in, "wide", axis=1, tiled=True),
        lax.all_gather(row_again[3], "wide", axis=1, tiled=True),
        lax.all_gather(row_again[4], "wide", axis=1, tiled=True),
    )
    b_enc_in, b_enc_mid, b_heads, b_dec_in, b_dec_mid, b_dec_out = back_full
    inv_count = 1.0 / count_all
    back_out = (keep * diff * jax.nn.sigmoid(out_pre) * inv_count).astype(jnp.bfloat16)
    out_bias_sum = jnp.sum(back_out.astype(jnp.float32), axis=0)
    grad_dec_out = contract_rows(back_out, hidden_four)
    back_four = jnp.dot(back_out, b_dec_out, preferred_element_type=jnp.float32)
    back_pre_four, gain_four, shift_four = norm_backward(
        back_four, normed_four, scaled_four, inverse_four, gain_rows[3], count_all
    )
    grad_dec_mid = contract_rows(hidden_three, back_pre_four)
    back_three = contract_cols(back_pre_four, b_dec_mid)
    back_pre_three, gain_three, shift_three = norm_backward(
        back_three, normed_three, scaled_three, inverse_three, gain_rows[2], count_all
    )
    grad_dec_in = contract_rows(code, back_pre_three)
    back_code = contract_cols(back_pre_three, b_dec_in)
    back_mean = back_code + ALPHA * latent_mean * inv_count
    back_logvar = (
        back_code * noise * spread_factor * 0.5 + ALPHA * 0.5 * (exp_logvar - 1.0) * inv_count
    )
    back_enc = jnp.concatenate([back_mean, back_logvar], axis=1).astype(jnp.bfloat16)
    head_bias_sum = jnp.sum(back_enc.astype(jnp.float32), axis=0)
    grad_heads = contract_rows(back_enc, hidden_two)
    back_two = jnp.dot(back_enc, b_heads, preferred_element_type=jnp.float32)
    back_pre_two, gain_two, shift_two = norm_backward(
        back_two, normed_two, scaled_two, inverse_two, gain_rows[1], count_all
    )
    grad_enc_mid = contract_rows(hidden_one, back_pre_two)
    back_one = contract_cols(back_pre_two, b_enc_mid)
    back_pre_one, gain_one, shift_one = norm_backward(
        back_one, normed_one, scaled_one, inverse_one, gain_rows[0], count_all
    )
    encoder_input_gradient = contract_rows(expression, back_pre_one)
    input_grad = contract_cols(back_pre_one, b_enc_in) * count_all - keep * diff
    row_split = lax.axis_size(("pair", "chip"))
    col_split = lax.axis_size("wide")
    full_grads = (encoder_input_gradient, grad_enc_mid, grad_heads, grad_dec_mid, grad_dec_out)
    block_list = [to_blocks(grad, row_split, col_split) for grad in full_grads]
    widths = [blk.shape[1] for blk in block_list]
    packed = jnp.concatenate(block_list, axis=1)
    mine = lax.psum_scatter(packed, ("wide", "pair", "chip"), scatter_dimension=0, tiled=True)[0]
    pieces = []
    offset = 0
    for grad, width in zip(full_grads, widths):
        block_shape = (grad.shape[0] // row_split, grad.shape[1] // col_split)
        pieces.append(mine[offset : offset + width].reshape(block_shape))
        offset = offset + width
    small = lax.psum(
        (grad_dec_in, head_bias_sum, out_bias_sum, loss_local), ("wide", "pair", "chip")
    )
    dec_in_full, head_bias_grad, out_bias_grad, loss_total = small
    wide_index = lax.axis_index("wide")
    col_count = dec_in_full.shape[1] // col_split
    row_index = lax.axis_index(("pair", "chip"))
    row_count = 8 // row_split
    dec_in_grad = lax.dynamic_slice_in_dim(dec_in_full, wide_index * col_count, col_count, 1)
    norm_full_grad = jnp.stack(
        [gain_one, gain_two, gain_three, gain_four, shift_one, shift_two, shift_three, shift_four]
    )
    norm_rows = lax.dynamic_slice_in_dim(norm_full_grad, row_index * row_count, row_count, 0)
    norm_grad = lax.dynamic_slice_in_dim(norm_rows, wide_index * col_count, col_count, 1)
    unbias = count_all / (count_all - 1.0)
    stats_full = jnp.stack(
        [
            centre_one,
            centre_two,
            centre_three,
            centre_four,
            spread_one * unbias,
            spread_two * unbias,
            spread_three * unbias,
            spread_four * unbias,
        ]
    )
    stats_rows = lax.dynamic_slice_in_dim(stats_full, row_index * row_count, row_count, 0)
    stats_mine = lax.dynamic_slice_in_dim(stats_rows, wide_index * col_count, col_count, 1)
    running_next = (1.0 - MOMENTUM) * running_stats + MOMENTUM * stats_mine
    loss = loss_total / count_all
    return (
        loss,
        input_grad,
        pieces[0],
        pieces[1],
        pieces[2],
        dec_in_grad,
        pieces[3],
        pieces[4],
        norm_grad,
        head_bias_grad,
        out_bias_grad,
        running_next,
    )


def solution(mesh):
    return jax.shard_map(
        on_device,
        mesh=mesh,
        in_specs=(
            P(("wide", "pair", "chip"), None),
            P(("wide", "pair", "chip"), None),
            P(("wide", "pair", "chip")),
            P(),
            P(("pair", "chip"), "wide"),
            P(("pair", "chip"), "wide"),
            P(("pair", "chip"), "wide"),
            P(None, "wide"),
            P(("pair", "chip"), "wide"),
            P(("pair", "chip"), "wide"),
            P(("pair", "chip"), "wide"),
            P(),
            P(),
            P(("pair", "chip"), "wide"),
        ),
        out_specs=(
            P(),
            P(("wide", "pair", "chip"), None),
            P(("pair", "chip"), "wide"),
            P(("pair", "chip"), "wide"),
            P(("pair", "chip"), "wide"),
            P(None, "wide"),
            P(("pair", "chip"), "wide"),
            P(("pair", "chip"), "wide"),
            P(("pair", "chip"), "wide"),
            P(),
            P(),
            P(("pair", "chip"), "wide"),
        ),
        check_vma=False,
    )
```

profile of v0, /device:TPU:0, one launch (start us, length us, event | category | flops | bytes accessed | tf_op | source)
XLA Modules:
  0.0 2043.9 jit_solution(11716391156971152103)
XLA Ops:
  8.7 35.0 %all-gather.22.cloned.1.call-done = bf16[8,875,200]{1,2,0:T(8,128)(2,1)} async-done(((bf16[1,875,200]{1,2,0:T(8,128)(2,1)}), bf16[8,875,200]{1,2,0:T(8,128)(2,1)}) %all-gather.22.cloned.1.call-update) | async-done | bytes 2800016 | tf_op jit(solution)/shard_map/all_gather | solution.py:80
  43.8 2.2 copy.40
  45.9 3.8 reshape.118
  49.9 11.1 all-gather.3
  62.2 9.2 all-gather.5
  72.6 5.8 all-gather.24.cloned.1.call-done
  78.4 2.2 copy.45
  80.6 3.9 reshape.130
  84.5 8.8 all-gather.1
  93.4 18.6 all-gather.2
  112.1 9.2 all-gather.4
  121.5 23.9 %all_gather.58 = bf16[100,800]{0,1:T(8,128)(2,1)S(1)} all-gather(bf16[100,200]{0,1:T(8,128)(2,1)S(1)} %copy-done.23), channel_id=1, replica_groups=mesh['wide'=4,'pair'=4,'chip'=2] {'wide'}, dimensions={1}, use_global_device_ids=true | all-gather | bytes 200000 | tf_op jit(solution)/shard_map/all_gather | solution.py:91
  146.6 21.5 %all_gather.57 = bf16[200,800]{0,1:T(8,128)(2,1)S(1)} all-gather(bf16[200,200]{0,1:T(8,128)(2,1)S(1)} %copy.43), channel_id=1, replica_groups=mesh['wide'=4,'pair'=4,'chip'=2] {'wide'}, dimensions={1}, use_global_device_ids=true | all-gather | bytes 400000 | tf_op jit(solution)/shard_map/all_gather | solution.py:90
  168.1 119.2 %all-gather.14.cloned.1.call-done = bf16[7000,800]{0,1:T(8,128)(2,1)} async-done(((bf16[7000,200]{0,1:T(8,128)(2,1)}), bf16[7000,800]{0,1:T(8,128)(2,1)}) %all-gather.14.cloned.1.call-update) | async-done | bytes 11200016 | tf_op jit(solution)/shard_map/all_gather | solution.py:88
  287.2 8.5 fusion.24
  295.8 39.8 %psum.140 = f32[800]{0:T(1024)S(1)} all-reduce(f32[800]{0:T(1024)S(1)} %get-tuple-element.89), channel_id=1, replica_groups=mesh['wide'=4,'pair'=4,'chip'=2] {'wide','pair','chip'}, use_global_device_ids=true, to_apply=%region_1.0 | all-reduce | flops 800 | bytes 6400 | tf_op jit(solution)/shard_map/psum | solution.py:32
  335.9 40.9 %psum.141 = f32[800]{0:T(1024)S(1)} all-reduce(f32[800]{0:T(1024)S(1)} %multiply_reduce_fusion.8), channel_id=1, replica_groups=mesh['wide'=4,'pair'=4,'chip'=2] {'wide','pair','chip'}, use_global_device_ids=true, to_apply=%region_3.0 | all-reduce | flops 800 | bytes 6400 | tf_op jit(solution)/shard_map/psum | solution.py:34
  377.4 2.4 fusion.25
  379.8 51.5 %psum.142 = f32[800]{0:T(1024)S(1)} all-reduce(f32[800]{0:T(1024)S(1)} %get-tuple-element.91), channel_id=1, replica_groups=mesh['wide'=4,'pair'=4,'chip'=2] {'wide','pair','chip'}, use_global_device_ids=true, to_apply=%region_5.6 | all-reduce | flops 800 | bytes 6400 | tf_op jit(solution)/shard_map/psum | solution.py:32
  431.6 46.4 %psum.143 = f32[800]{0:T(1024)S(1)} all-reduce(f32[800]{0:T(1024)S(1)} %multiply_reduce_fusion.7), channel_id=1, replica_groups=mesh['wide'=4,'pair'=4,'chip'=2] {'wide','pair','chip'}, use_global_device_ids=true, to_apply=%region_7.8 | all-reduce | flops 800 | bytes 6400 | tf_op jit(solution)/shard_map/psum | solution.py:34
  480.5 46.0 %psum.144 = f32[800]{0:T(1024)S(1)} all-reduce(f32[800]{0:T(1024)S(1)} %get-tuple-element.93), channel_id=1, replica_groups=mesh['wide'=4,'pair'=4,'chip'=2] {'wide','pair','chip'}, use_global_device_ids=true, to_apply=%region_9.10 | all-reduce | flops 800 | bytes 6400 | tf_op jit(solution)/shard_map/psum | solution.py:32
  526.8 45.3 %psum.145 = f32[800]{0:T(1024)S(1)} all-reduce(f32[800]{0:T(1024)S(1)} %multiply_reduce_fusion.6), channel_id=1, replica_groups=mesh['wide'=4,'pair'=4,'chip'=2] {'wide','pair','chip'}, use_global_device_ids=true, to_apply=%region_11.12 | all-reduce | flops 800 | bytes 6400 | tf_op jit(solution)/shard_map/psum | solution.py:34
  572.8 3.0 fusion.27
  575.8 39.4 %psum.146 = f32[800]{0:T(1024)} all-reduce(f32[800]{0:T(1024)} %get-tuple-element.95), channel_id=1, replica_groups=mesh['wide'=4,'pair'=4,'chip'=2] {'wide','pair','chip'}, use_global_device_ids=true, to_apply=%region_13.14 | all-reduce | flops 800 | bytes 6400 | tf_op jit(solution)/shard_map/psum | solution.py:32
  617.4 41.7 %psum.147 = f32[800]{0:T(1024)} all-reduce(f32[800]{0:T(1024)} %multiply_reduce_fusion.5), channel_id=1, replica_groups=mesh['wide'=4,'pair'=4,'chip'=2] {'wide','pair','chip'}, use_global_device_ids=true, to_apply=%region_15.16 | all-reduce | flops 800 | bytes 6400 | tf_op jit(solution)/shard_map/psum | solution.py:34
  660.4 10.4 convolution_add_fusion
  670.9 10.5 convert_reduce_fusion
  681.4 10.1 fusion.23
  691.5 39.9 %all-reduce.4 = (f32[800]{0:T(1024)}, f32[800]{0:T(1024)}) all-reduce(f32[800]{0:T(1024)} %get-tuple-element.47, f32[800]{0:T(1024)} %get-tuple-element.46), channel_id=1, replica_groups=mesh['wide'=4,'pair'=4,'chip'=2] {'wide','pair','chip'}, use_global_device_ids=true, to_apply=%region_23.24 | all-reduce | flops 1600 | bytes 12800 | tf_op jit(solution)/shard_map/psum | solution.py:51
  732.7 4.8 fusion.22
  737.5 41.5 %all-reduce.3 = (f32[800]{0:T(1024)}, f32[800]{0:T(1024)}) all-reduce(f32[800]{0:T(1024)} %get-tuple-element.45, f32[800]{0:T(1024)} %get-tuple-element.44), channel_id=1, replica_groups=mesh['wide'=4,'pair'=4,'chip'=2] {'wide','pair','chip'}, use_global_device_ids=true, to_apply=%region_27.28 | all-reduce | flops 1600 | bytes 12800 | tf_op jit(solution)/shard_map/psum | solution.py:51
  779.8 1.7 multiply_convert_fusion.3
  781.6 1.8 add_convert_fusion.1
  783.4 2.7 fusion.21
  787.5 3.0 fusion.18
  790.6 9.3 fusion.15
  801.0 39.7 %all-reduce.2 = (f32[800]{0:T(1024)S(1)}, f32[800]{0:T(1024)S(1)}) all-reduce(f32[800]{0:T(1024)S(1)} %get-tuple-element.43, f32[800]{0:T(1024)S(1)} %get-tuple-element.42), channel_id=1, replica_groups=mesh['wide'=4,'pair'=4,'chip'=2] {'wide','pair','chip'}, use_global_device_ids=true, to_apply=%region_31.32 | all-reduce | flops 1600 | bytes 12800 | tf_op jit(solution)/shard_map/psum | solution.py:51
  841.3 4.2 fusion.16
  845.5 3.2 fusion.20
  848.8 42.1 %all-reduce.1 = (f32[]{:T(128)}, f32[800]{0:T(1024)S(1)}, f32[800]{0:T(1024)S(1)}, f32[200]{0:T(256)}, f32[7000]{0:T(1024)}) all-reduce(f32[]{:T(128)} %add_reduce_fusion, f32[800]{0:T(1024)S(1)} %get-tuple-element.41, f32[800]{0:T(1024)S(1)} %get-tuple-element.40, ...), channel_id=1, replica_groups=mesh['wide'=4,'pair'=4,'chip'=2] {'wide','pair','chip'}, use_global_device_ids=true, to_apply=%region_19.20 | all-reduce | flops 8801 | bytes 70408 | tf_op jit(solution)/shard_map/psum | solution.py:200
  890.8 11.4 convolution_bitcast_fusion
  902.2 25.9 %reshape.102 = f32[8,875,4,200]{1,0,3,2:T(8,128)} reshape(f32[7000,800]{0,1:T(8,128)} %convolution_bitcast_fusion) | data formatting | bytes 44800000 | tf_op jit(solution)/shard_map/reshape | solution.py:25
  928.1 29.9 %copy.46 = f32[8,875,4,200]{3,1,0,2:T(8,128)} copy(f32[8,875,4,200]{1,0,3,2:T(8,128)} %reshape.102) | data formatting | bytes 44800000 | tf_op jit(solution)/shard_map/reshape | solution.py:25
  958.0 53.5 %reshape.103 = f32[32,175000]{1,0:T(8,128)} reshape(f32[4,8,875,200]{3,2,1,0:T(8,128)} %bitcast.63) | data formatting | bytes 44800000 | tf_op jit(solution)/shard_map/reshape | solution.py:26
  1011.5 3.8 reshape.104
  1015.3 2.6 copy.61
  1017.9 2.4 reshape.105
  1020.3 1.8 reshape.106
  1023.6 5.8 reshape.108
  1029.5 2.6 copy.60
  1032.0 2.5 reshape.109
  1034.5 25.9 %reshape.110 = f32[8,875,4,200]{1,0,3,2:T(8,128)} reshape(f32[7000,800]{0,1:T(8,128)} %fusion.15) | data formatting | bytes 44800000 | tf_op jit(solution)/shard_map/reshape | solution.py:25
  1060.4 29.9 %copy.50 = f32[8,875,4,200]{3,1,0,2:T(8,128)} copy(f32[8,875,4,200]{1,0,3,2:T(8,128)} %reshape.110) | data formatting | bytes 44800000 | tf_op jit(solution)/shard_map/reshape | solution.py:25
  1090.2 53.1 %reshape.111 = f32[32,175000]{1,0:T(8,128)} reshape(f32[4,8,875,200]{3,2,1,0:T(8,128)} %bitcast.64) | data formatting | bytes 44800000 | tf_op jit(solution)/shard_map/reshape | solution.py:26
  1143.4 56.1 %dynamic-update-slice = f32[32,395000]{1,0:T(8,128)} dynamic-update-slice(f32[32,395000]{1,0:T(8,128)} %custom-call, f32[32,175000]{1,0:T(8,128)} %reshape.103, s32[]{} %constant.134, s32[]{} %constant.134) | dynamic-update-slice | bytes 44800004
  1199.5 8.9 dynamic-update-slice.1
  1208.4 3.8 dynamic-update-slice.2
  1212.2 9.4 dynamic-update-slice.3
  1221.6 62.1 %dynamic-update-slice.4 = f32[32,395000]{1,0:T(8,128)} dynamic-update-slice(f32[32,395000]{1,0:T(8,128)} %dynamic-update-slice.3, f32[32,175000]{1,0:T(8,128)} %reshape.111, s32[]{} %constant.134, s32[]{} %constant.138) | dynamic-update-slice | bytes 44800004 | tf_op jit(solution)/shard_map/concatenate | solution.py:192
  1286.7 16.5 fusion
  1303.2 710.2 %all-reduce.8.cloned.1.call-done = (f32[32,395000]{1,0:T(8,128)}, f32[100,800]{0,1:T(8,128)}) async-done(((f32[32,395000]{1,0:T(8,128)}, f32[100,800]{0,1:T(8,128)}), (f32[32,395000]{1,0:T(8,128)}, f32[100,800]{0,1:T(8,128)})) %all-reduce.8.cloned.1.call-update) | async-done | bytes 50880016
  2013.4 10.3 dynamic-slice_reduce_fusion
  2026.1 1.8 dynamic-slice_reduce_fusion.2
  2030.6 1.5 constant_dynamic-slice_fusion
  (222 shorter events, 30.8 us)
Async XLA Ops:
  7.2 36.6 %all-gather.22.cloned.1.call-start = ((), (), s32[]{:S(2)}) async-start(), calls=%async_computation.4 | async-start | bytes 3225600 | tf_op jit(solution)/shard_map/all_gather | solution.py:80
  7.9 70.5 %all-gather.24.cloned.1.call-start = ((), (), s32[]{:S(2)}) async-start(), calls=%async_computation.5 | async-start | bytes 3225600 | tf_op jit(solution)/shard_map/all_gather | solution.py:84
  8.7 41.2 %copy-start.21 = (bf16[100,200]{0,1:T(8,128)(2,1)S(1)}, bf16[100,200]{0,1:T(8,128)(2,1)}, u32[]{:S(2)}) copy-start(bf16[100,200]{0,1:T(8,128)(2,1)} %param.19) | copy-start | bytes 120004
  8.7 53.5 %copy-start.22 = (bf16[100,200]{0,1:T(8,128)(2,1)S(1)}, bf16[100,200]{0,1:T(8,128)(2,1)}, u32[]{:S(2)}) copy-start(bf16[100,200]{0,1:T(8,128)(2,1)} %param.22) | copy-start | bytes 120004
  8.7 278.6 %all-gather.14.cloned.1.call-start = ((), (), s32[]{:S(2)}) async-start(), calls=%async_computation | async-start | bytes 14080000 | tf_op jit(solution)/shard_map/all_gather | solution.py:88
  49.8 327.6 %all-gather.16.cloned.1.call-start = ((), (), s32[]{:S(2)}) async-start(), calls=%async_computation.1 | async-start | bytes 1792000 | tf_op jit(solution)/shard_map/all_gather | solution.py:89
  62.2 510.6 %all-gather.18.cloned.1.call-start = ((), (), s32[]{:S(2)}) async-start(), calls=%async_computation.2 | async-start | bytes 1792000 | tf_op jit(solution)/shard_map/all_gather | solution.py:92
  72.5 12.0 copy-start.60
  72.6 39.5 %copy-start.37 = (bf16[25,200]{1,0:T(8,128)(2,1)S(1)}, bf16[25,200]{1,0:T(8,128)(2,1)}, u32[]{:S(2)}) copy-start(bf16[25,200]{1,0:T(8,128)(2,1)} %param.20) | copy-start | bytes 30004
  72.6 48.9 %copy-start.23 = (bf16[100,200]{0,1:T(8,128)(2,1)S(1)}, bf16[100,200]{0,1:T(8,128)(2,1)}, u32[]{:S(2)}) copy-start(bf16[100,200]{0,1:T(8,128)(2,1)} %param.21) | copy-start | bytes 120004
  72.6 587.8 %all-gather.20.cloned.1.call-start = ((), (), s32[]{:S(2)}) async-start(), calls=%async_computation.3 | async-start | bytes 14080000 | tf_op jit(solution)/shard_map/all_gather | solution.py:93
  84.5 1928.9 %all-reduce.8.cloned.1.call-start = ((), (), s32[]{:S(2)}) async-start(), calls=%async_computation.6 | async-start | bytes 101941248
  145.3 334.8 %copy-start.13 = (bf16[100,800]{0,1:T(8,128)(2,1)}, bf16[100,800]{0,1:T(8,128)(2,1)S(1)}, u32[]{:S(2)}) copy-start(bf16[100,800]{0,1:T(8,128)(2,1)S(1)} %all_gather.58) | copy-start | bytes 480004
  146.0 231.4 %copy-start.50 = (f32[800]{0:T(1024)}, f32[800]{0:T(1024)S(1)}, u32[]{:S(2)}) copy-start(f32[800]{0:T(1024)S(1)} %get-tuple-element.55) | copy-start | bytes 9604
  146.0 332.6 %copy-start.30 = (f32[800]{0:T(1024)}, f32[800]{0:T(1024)S(1)}, u32[]{:S(2)}) copy-start(f32[800]{0:T(1024)S(1)} %get-tuple-element.54) | copy-start | bytes 9604
  146.6 230.8 %copy-start.38 = (f32[800]{0:T(1024)}, f32[800]{0:T(1024)S(1)}, u32[]{:S(2)}) copy-start(f32[800]{0:T(1024)S(1)} %get-tuple-element.51) | copy-start | bytes 9604
  146.6 332.0 %copy-start.26 = (f32[800]{0:T(1024)}, f32[800]{0:T(1024)S(1)}, u32[]{:S(2)}) copy-start(f32[800]{0:T(1024)S(1)} %get-tuple-element.50) | copy-start | bytes 9604
  146.6 425.5 %copy-start.40 = (f32[800]{0:T(1024)}, f32[800]{0:T(1024)S(1)}, u32[]{:S(2)}) copy-start(f32[800]{0:T(1024)S(1)} %get-tuple-element.49) | copy-start | bytes 9604
  295.8 595.1 %copy-start.1 = (f32[256,800]{0,1:T(8,128)}, f32[256,800]{0,1:T(8,128)S(1)}, u32[]{:S(2)}) copy-start(f32[256,800]{0,1:T(8,128)S(1)} %get-tuple-element.90) | copy-start | bytes 2457604
  295.8 183.9 %copy-start.59 = (f32[200]{0:T(256)S(1)}, f32[200]{0:T(256)}, u32[]{:S(2)}) copy-start(f32[200]{0:T(256)} %param.25) | copy-start | bytes 2404
  295.8 184.3 %copy-start.14 = (f32[256,100]{0,1:T(8,128)S(1)}, f32[256,100]{0,1:T(8,128)}, u32[]{:S(2)}) copy-start(f32[256,100]{0,1:T(8,128)} %param.15) | copy-start | bytes 307204
  379.8 100.3 %copy-start.8 = (f32[256,800]{0,1:T(8,128)}, f32[256,800]{0,1:T(8,128)S(1)}, u32[]{:S(2)}) copy-start(f32[256,800]{0,1:T(8,128)S(1)} %get-tuple-element.92) | copy-start | bytes 2457604
  526.5 260.9 %copy-start.15 = (f32[800]{0:T(1024)}, f32[800]{0:T(1024)S(1)}, u32[]{:S(2)}) copy-start(f32[800]{0:T(1024)S(1)} %broadcast_multiply_fusion.9) | copy-start | bytes 9604
  660.4 10.4 copy-start.7
  660.4 10.4 copy-start.64
  660.4 10.4 copy-start.65
  670.8 10.5 copy-start.18
  670.8 10.5 copy-start.24
  670.9 10.5 copy-start.28
  670.9 10.5 copy-start.34
  681.3 10.2 copy-start.3
  779.0 8.5 copy-start.19
  779.0 8.5 copy-start.33
  779.0 8.5 copy-start.35
  779.0 8.5 copy-start.41
  779.0 8.5 copy-start.52
  779.0 8.5 copy-start.54
  779.0 8.5 copy-start.56
  779.0 8.5 copy-start.57
  779.0 8.5 copy-start.66
  783.4 7.2 copy-start.4
  783.4 7.2 copy-start.25
  783.4 7.2 copy-start.29
  790.5 50.1 %copy-start.61 = (f32[256]{0:T(256)S(1)}, f32[256]{0:T(256)}, u32[]{:S(2)}) copy-start(f32[256]{0:T(256)} %get-tuple-element.71) | copy-start | bytes 3076
  790.6 50.1 %copy-start.62 = (f32[256]{0:T(256)S(1)}, f32[256]{0:T(256)}, u32[]{:S(2)}) copy-start(f32[256]{0:T(256)} %get-tuple-element.74) | copy-start | bytes 3076
  790.6 50.7 %copy-start.9 = (f32[256,800]{0,1:T(8,128)S(1)}, f32[256,800]{0,1:T(8,128)}, u32[]{:S(2)}) copy-start(f32[256,800]{0,1:T(8,128)} %copy-done.8) | copy-start | bytes 2457604
  790.6 50.7 %copy-start.32 = (f32[800]{0:T(1024)S(1)}, f32[800]{0:T(1024)}, u32[]{:S(2)}) copy-start(f32[800]{0:T(1024)} %copy-done.31) | copy-start | bytes 9604
  790.6 50.7 %copy-start.39 = (f32[800]{0:T(1024)S(1)}, f32[800]{0:T(1024)}, u32[]{:S(2)}) copy-start(f32[800]{0:T(1024)} %copy-done.38) | copy-start | bytes 9604
  790.6 50.7 %copy-start.51 = (f32[800]{0:T(1024)S(1)}, f32[800]{0:T(1024)}, u32[]{:S(2)}) copy-start(f32[800]{0:T(1024)} %copy-done.50) | copy-start | bytes 9604
  790.6 50.7 %copy-start.53 = (f32[800]{0:T(1024)S(1)}, f32[800]{0:T(1024)}, u32[]{:S(2)}) copy-start(f32[800]{0:T(1024)} %get-tuple-element.84) | copy-start | bytes 9604
  800.0 45.5 %copy-start.10 = (f32[256,800]{0,1:T(8,128)S(1)}, f32[256,800]{0,1:T(8,128)}, u32[]{:S(2)}) copy-start(f32[256,800]{0,1:T(8,128)} %copy-done.8) | copy-start | bytes 2457604
  800.0 45.5 %copy-start.67 = (f32[256,800]{0,1:T(8,128)S(1)}, f32[256,800]{0,1:T(8,128)}, u32[]{:S(2)}) copy-start(f32[256,800]{0,1:T(8,128)} %get-tuple-element.100) | copy-start | bytes 2457604
  840.7 8.1 copy-start.48
  841.3 7.5 copy-start.27
  848.7 53.5 %copy-start.5 = (f32[256,800]{0,1:T(8,128)}, f32[256,800]{0,1:T(8,128)S(1)}, u32[]{:S(2)}) copy-start(f32[256,800]{0,1:T(8,128)S(1)} %get-tuple-element.101) | copy-start | bytes 2457604
  958.0 53.5 %copy-start.11 = (f32[800,800]{1,0:T(8,128)S(1)}, f32[800,800]{1,0:T(8,128)}, u32[]{:S(2)}) copy-start(f32[800,800]{1,0:T(8,128)} %fusion.16) | copy-start | bytes 7680004
  1143.4 56.1 %copy-start = (f32[32,20000]{1,0:T(8,128)S(1)}, f32[32,20000]{1,0:T(8,128)}, u32[]{:S(2)}) copy-start(f32[32,20000]{1,0:T(8,128)} %reshape.105) | copy-start | bytes 7680004
  1143.4 65.0 %copy-start.12 = (f32[32,5000]{1,0:T(8,128)S(1)}, f32[32,5000]{1,0:T(8,128)}, u32[]{:S(2)}) copy-start(f32[32,5000]{1,0:T(8,128)} %reshape.107) | copy-start | bytes 1920004
  1283.8 0.8 copy-start.43
  1283.8 0.8 copy-start.44
  1283.8 0.8 copy-start.45
  1283.8 2.2 copy-start.63
  1283.9 2.9 copy-start.2
  1283.9 2.9 copy-start.6
  (11 other events, 7.5 us)
Sparse Core Ops, SparseCore 0:
  9.9 33.8 all-gather.21
  45.7 32.7 all-gather.23
  80.6 206.6 all-gather.13
  289.2 33.7 all-gather.15
  325.0 34.3 all-gather.17
  360.9 199.5 all-gather.19
  1284.0 729.3 all-reduce.7
where the time goes:
time: 2060 us; the launch traced here: 2040 us
  waiting for transfers between devices  872 us (42%)
  blocking collectives  616 us (30%)
  local copies, waits for them, and re-layouts  423 us (21%)
  matrix products  105 us (5%)
    unnamed x8, waiting for transfers between devices  712 us
    psum x4, blocking collectives, batch_moments(): lax.psum(jnp.sum(pre_act, axis=0), ('wide', 'pair', 'chip')) / count_all  177 us
    psum x4, blocking collectives, batch_moments(): lax.psum(jnp.sum(jnp.square(pre_act - centre), axis=0), ('wide', 'pair',...  174 us
    reshape x10, local copies, waits for them, and re-layouts, to_blocks(): grad.reshape(row_parts, rows // row_parts, col_parts, cols // col_parts)  128 us
    psum x3, blocking collectives, norm_backward(): lax.psum((jnp.sum(back_normed, axis=0), jnp.sum(back_normed * scaled, axi...  121 us
    all_gather x1, waiting for transfers between devices, on_device(): lax.all_gather(row_parts[0], 'wide', axis=1, tiled=True)  119 us
    reshape x5, local copies, waits for them, and re-layouts, to_blocks(): shaped.transpose(2, 0, 1, 3)  113 us
    unnamed x152, local copies, waits for them, and re-layouts  94.6 us
  transfers between devices with their start and end apart: 7, of which 4 were waited for; matrix products, arithmetic and copies ran while one was open for 3% of the time, Pallas kernels for 0%

commit v1 on v0

v1 whole, which is shorter than its diff:
```python
import jax
import jax.numpy as jnp
from jax import lax
from jax.sharding import PartitionSpec as P

ALPHA = 0.005
EPSILON = 1e-05
MOMENTUM = 0.1
LONGEST_RING = 8
ALL = ("wide", "pair", "chip")
BF = jnp.bfloat16
F32 = jnp.float32


def dot(left, right, dims):
    return lax.dot_general(left, right, (dims, ((), ())), preferred_element_type=F32)


def nn(left, right):
    return dot(left, right, ((1,), (0,)))


def nt(left, right):
    return dot(left, right, ((1,), (1,)))


def tn(left, right):
    return dot(left, right, ((0,), (0,)))


def swap_pair(value, bits):
    count = lax.axis_size("pair")
    return lax.ppermute(value, "pair", [(i, i ^ bits) for i in range(count)])


def swap_chip(value):
    return lax.ppermute(value, "chip", [(0, 1), (1, 0)])


def next_wide(value):
    count = lax.axis_size("wide")
    return lax.ppermute(value, "wide", [(i, (i + 1) % count) for i in range(count)])


def half_of(units):
    return max(units // 2 // 8 * 8, 1)


def spread_pair(block):
    cut = half_of(block.shape[0])
    by_x = swap_pair(block, 1)
    by_y = swap_pair(block, 2)
    upper = swap_pair(by_y[:cut], 1)
    lower = swap_pair(by_x[cut:], 2)
    return [block, by_x, by_y, jnp.concatenate([upper, lower], axis=0)]


def gather_ring(block):
    count = lax.axis_size("wide")
    if count > LONGEST_RING:
        line = lax.all_gather(block, "wide", axis=0, tiled=True)
        spread = [jnp.split(item, count) for item in spread_pair(jnp.concatenate(mirror(line)))]
        return list(zip(*spread))
    ring = [block]
    for _ in range(count - 1):
        ring.append(next_wide(ring[-1]))
    return [spread_pair(item) for item in ring]


def sum_pair(parts):
    own, for_x, for_y, for_diag = parts
    cut = half_of(own.shape[0])
    diag = for_diag.astype(BF)
    upper = swap_pair(diag[:cut], 1)
    lower = swap_pair(diag[cut:], 2)
    for_y = jnp.concatenate([for_y[:cut] + upper.astype(F32), for_y[cut:]], axis=0).astype(BF)
    for_x = jnp.concatenate([for_x[:cut], for_x[cut:] + lower.astype(F32)], axis=0).astype(BF)
    from_x = swap_pair(for_x, 1)
    from_y = swap_pair(for_y, 2)
    return own + from_x.astype(F32) + from_y.astype(F32)


def scatter_ring(make_parts):
    count = lax.axis_size("wide")
    if count > LONGEST_RING:
        parts = [jnp.concatenate(item) for item in zip(*[make_parts(s) for s in range(count)])]
        line = jnp.concatenate(mirror(sum_pair(parts))).astype(BF)
        return lax.psum_scatter(line, "wide", scatter_dimension=0, tiled=True).astype(F32)
    total = sum_pair(make_parts(1 % count))
    for step in range(2, count + 1):
        arrived = next_wide(total.astype(BF))
        total = sum_pair(make_parts(step % count)) + arrived.astype(F32)
    return total


def mirror(value):
    count = lax.axis_size("wide")
    me = lax.axis_index("wide")
    shaped = value.reshape((count, value.shape[0] // count) + value.shape[1:])
    return [
        lax.dynamic_index_in_dim(shaped, lax.rem(me - s + count, count), 0, keepdims=False)
        for s in range(count)
    ]


def share(value):
    count = lax.axis_size(ALL)
    return lax.all_to_all(
        jnp.broadcast_to(value[None], (count,) + value.shape), ALL, 0, 0, tiled=True
    )


def normalize(pre_act, gain, shift):
    cells = pre_act.shape[1]
    count = lax.axis_size(ALL)
    local_mean = jnp.mean(pre_act, axis=1)
    local_square = jnp.sum(jnp.square(pre_act - local_mean[:, None]), axis=1)
    every = share(jnp.stack([local_mean, local_square]))
    centre = jnp.mean(every[:, 0], axis=0)
    squares = jnp.sum(every[:, 1], axis=0) + cells * jnp.sum(
        jnp.square(every[:, 0] - centre), axis=0
    )
    variance = squares / (cells * count)
    inverse = lax.rsqrt(variance + EPSILON)
    scaled = (pre_act - centre[:, None]) * inverse[:, None]
    normed = scaled * gain[:, None] + shift[:, None]
    return normed, scaled, inverse, centre, variance


def norm_backward(upstream, normed, scaled, inverse, gain, extra=None):
    count_all = upstream.shape[1] * lax.axis_size(ALL)
    gate = jax.nn.sigmoid(normed)
    back_normed = upstream * gate * (1.0 + normed * (1.0 - gate))
    sums = jnp.stack([jnp.sum(back_normed, axis=1), jnp.sum(back_normed * scaled, axis=1)])
    if extra is not None:
        sums = jnp.concatenate([sums.reshape(-1), extra])
    every = jnp.sum(share(sums), axis=0)
    units = upstream.shape[0]
    flat = every.reshape(-1)
    shift_sum, gain_sum = flat[:units], flat[units : 2 * units]
    back_pre = (gain * inverse)[:, None] * (
        back_normed - shift_sum[:, None] / count_all - scaled * (gain_sum / count_all)[:, None]
    )
    return back_pre.astype(BF), gain_sum, shift_sum, flat[2 * units :]


def on_device(
    expression,
    noise,
    study,
    measured_gene_mask,
    encoder_input_weight,
    enc_mid,
    heads,
    dec_in,
    dec_mid,
    dec_out,
    norm_params,
    head_bias,
    out_bias,
    running_stats,
):
    wide_count = lax.axis_size("wide")
    row_split = lax.axis_size(("pair", "chip"))
    pair_count = lax.axis_size("pair")
    cells, genes = expression.shape
    count_all = cells * lax.axis_size(ALL)
    inv_count = 1.0 / count_all
    latent = dec_in.shape[0]
    block_genes, block_units = encoder_input_weight.shape
    units = block_units * wide_count
    pair = lax.axis_index("pair")
    chip = lax.axis_index("chip")
    block_id = pair * 2 + chip

    enc_blocks = gather_ring(encoder_input_weight.T)

    piece = -(-latent // row_split)
    piece_start = jnp.minimum(piece * block_id, latent - piece)
    dec_in_piece = lax.dynamic_slice_in_dim(dec_in, piece_start, piece, 0)
    packed = jnp.concatenate(
        [enc_mid.T, dec_mid.T, heads.T, dec_in_piece.T, norm_params.T], axis=1
    )
    mine = lax.all_gather(packed, ("wide", "pair"))
    other = swap_chip(mine)
    first = jnp.where(chip == 0, mine, other)
    second = jnp.where(chip == 0, other, mine)
    mid = jnp.stack([first, second], axis=1)
    mid = mid.reshape(wide_count, row_split, block_units, packed.shape[1])
    mid_rows = enc_mid.shape[0]
    head_rows = heads.shape[0]

    def pick(start, size):
        part = mid[:, :, :, start : start + size]
        return part.transpose(0, 2, 1, 3).reshape(units, row_split * size)

    w_enc_mid = pick(0, mid_rows)
    w_dec_mid = pick(mid_rows, mid_rows)
    w_heads = pick(2 * mid_rows, head_rows)
    in_all = pick(2 * mid_rows + head_rows, piece)
    lead = piece * (row_split - 1)
    w_dec_in = jnp.concatenate(
        [in_all[:, :lead], in_all[:, row_split * piece - (latent - lead) :]], axis=1
    )
    norm_full = pick(2 * mid_rows + head_rows + piece, 1).astype(F32)
    gains = [norm_full[:, k] for k in range(4)]
    shifts = [norm_full[:, 4 + k] for k in range(4)]

    by_block = expression.T.reshape(pair_count, 2, block_genes, cells)

    def block_pair(rel, which):
        return lax.dynamic_slice(
            by_block, (pair ^ rel, which, 0, 0), (1, 1, block_genes, cells)
        ).reshape(block_genes, cells)

    x_mine = [block_pair(rel, chip) for rel in range(pair_count)]
    x_send = jnp.stack([block_pair(rel, 1 - chip) for rel in range(pair_count)])
    x_recv = swap_chip(x_send)
    x_chip = [jnp.concatenate([x_mine[r], x_recv[r]], axis=1) for r in range(pair_count)]

    labels = measured_gene_mask.shape[0]
    indicator = (jnp.arange(labels, dtype=jnp.int32)[:, None] == study[None, :]).astype(BF)
    indicator = jnp.concatenate([indicator, swap_chip(indicator)], axis=1)

    rel_pre = []
    for s in range(wide_count):
        rel_pre.append(sum(nn(enc_blocks[s][r], x_chip[r]) for r in range(pair_count)))
    part_one = jnp.concatenate(rel_pre, axis=0)
    pre_one = part_one[:, :cells] + swap_chip(part_one[:, cells:])
    pre_one = jnp.concatenate(mirror(pre_one), axis=0)
    normed_one, scaled_one, inverse_one, centre_one, spread_one = normalize(
        pre_one, gains[0], shifts[0]
    )
    hidden_one = jax.nn.silu(normed_one).astype(BF)

    dec_blocks = gather_ring(lax.optimization_barrier((dec_out.T, rel_pre[-1]))[0])

    pre_two = nn(w_enc_mid, hidden_one)
    normed_two, scaled_two, inverse_two, centre_two, spread_two = normalize(
        pre_two, gains[1], shifts[1]
    )
    hidden_two = jax.nn.silu(normed_two).astype(BF)
    encoded = tn(w_heads, hidden_two) + head_bias[:, None]
    latent_mean = encoded[:latent]
    logvar = encoded[latent:]
    noise_t = noise.T
    spread_factor = jnp.exp(0.5 * logvar)
    code = (latent_mean + spread_factor * noise_t).astype(BF)
    pre_three = nn(w_dec_in, code)
    normed_three, scaled_three, inverse_three, centre_three, spread_three = normalize(
        pre_three, gains[2], shifts[2]
    )
    hidden_three = jax.nn.silu(normed_three).astype(BF)
    pre_four = nn(w_dec_mid, hidden_three)
    normed_four, scaled_four, inverse_four, centre_four, spread_four = normalize(
        pre_four, gains[3], shifts[3]
    )
    hidden_four = jax.nn.silu(normed_four).astype(BF)

    h_chip = mirror(jnp.concatenate([hidden_four, swap_chip(hidden_four)], axis=1))
    h_rel = jnp.concatenate(h_chip, axis=0)
    recon_sum = 0.0
    back_out = []
    kept_diff = []
    bias_sums = []
    back_rel = 0.0
    for r in range(pair_count):
        start = ((pair ^ r) * 2 + chip) * block_genes
        w_r = jnp.concatenate([dec_blocks[s][r] for s in range(wide_count)], axis=0)
        bias_r = lax.dynamic_slice_in_dim(out_bias, start, block_genes, 0)
        mask_r = lax.dynamic_slice_in_dim(measured_gene_mask, start, block_genes, 1).astype(BF)
        keep = tn(mask_r, indicator)
        out_pre = tn(w_r, h_rel) + bias_r[:, None]
        small = jnp.exp(-jnp.abs(out_pre))
        recon = jnp.maximum(out_pre, 0.0) + jnp.log1p(small)
        gate = jnp.where(out_pre >= 0, 1.0, small) / (1.0 + small)
        diff = recon - x_chip[r].astype(F32)
        kd = keep * diff
        recon_sum = recon_sum + jnp.sum(kd * diff)
        b_r = (kd * gate * inv_count).astype(BF)
        bias_sums.append(jnp.sum(b_r.astype(F32), axis=1))
        back_out.append(b_r)
        kept_diff.append(kd)
        back_rel = back_rel + nn(w_r, b_r)
    exp_logvar = jnp.exp(logvar)
    kl_sum = jnp.sum(exp_logvar + latent_mean * latent_mean - 1.0 - logvar)
    loss_local = 0.5 * recon_sum + (0.5 * ALPHA) * kl_sum

    back_four = back_rel[:, :cells] + swap_chip(back_rel[:, cells:])
    back_four = jnp.concatenate(mirror(back_four), axis=0)

    bias_rows = jnp.zeros((row_split, block_genes), F32)
    for r in range(pair_count):
        bias_rows = lax.dynamic_update_slice_in_dim(
            bias_rows, bias_sums[r][None], (pair ^ r) * 2 + chip, 0
        )
    bp_four, gain_four, shift_four, rest = norm_backward(
        back_four,
        normed_four,
        scaled_four,
        inverse_four,
        gains[3],
        jnp.concatenate([bias_rows.reshape(-1), loss_local[None]]),
    )
    out_bias_grad = rest[:genes]
    loss = rest[genes] * inv_count

    dec_out_grad = scatter_ring(
        lambda s: [nt(h_chip[s], back_out[r]) for r in range(pair_count)]
    )

    grad_dec_mid = nt(bp_four, hidden_three)
    back_three = tn(w_dec_mid, bp_four)
    bp_three, gain_three, shift_three, _ = norm_backward(
        back_three, normed_three, scaled_three, inverse_three, gains[2]
    )
    grad_dec_in = nt(bp_three, code)
    back_code = tn(w_dec_in, bp_three)
    back_mean = back_code + ALPHA * inv_count * latent_mean
    back_logvar = (
        back_code * noise_t * spread_factor * 0.5
        + (ALPHA * 0.5 * inv_count) * (exp_logvar - 1.0)
    )
    back_enc = jnp.concatenate([back_mean, back_logvar], axis=0).astype(BF)
    head_sum = jnp.sum(back_enc.astype(F32), axis=1)
    grad_heads = nt(hidden_two, back_enc)
    back_two = nn(w_heads, back_enc)
    bp_two, gain_two, shift_two, head_bias_grad = norm_backward(
        back_two, normed_two, scaled_two, inverse_two, gains[1], head_sum
    )
    grad_enc_mid = nt(bp_two, hidden_one)
    back_one = tn(w_enc_mid, bp_two)
    bp_one, gain_one, shift_one, _ = norm_backward(
        back_one, normed_one, scaled_one, inverse_one, gains[0]
    )

    d_chip = mirror(jnp.concatenate([bp_one, swap_chip(bp_one)], axis=1))
    enc_in_grad = scatter_ring(lambda s: [nt(d_chip[s], x_chip[r]) for r in range(pair_count)])
    d_rel = jnp.concatenate(d_chip, axis=0)
    own_rows = []
    other_rows = []
    for r in range(pair_count):
        w_r = jnp.concatenate([enc_blocks[s][r] for s in range(wide_count)], axis=0)
        grad_r = tn(w_r, d_rel) * count_all - kept_diff[r]
        own_rows.append(grad_r[:, :cells])
        other_rows.append(grad_r[:, cells:].astype(BF))
    came = swap_chip(jnp.stack(other_rows))
    rows = jnp.zeros((row_split, block_genes, cells), F32)
    for r in range(pair_count):
        base = (pair ^ r) * 2
        rows = lax.dynamic_update_slice_in_dim(rows, own_rows[r][None], base + chip, 0)
        rows = lax.dynamic_update_slice_in_dim(
            rows, came[r][None].astype(F32), base + 1 - chip, 0
        )
    input_grad = rows.reshape(genes, cells).T

    def to_blocks(grad, width):
        return grad.reshape(wide_count, block_units, row_split, width).transpose(0, 2, 1, 3)

    pad = piece * row_split - latent
    dec_in_wide = jnp.pad(grad_dec_in, ((0, 0), (0, pad)))
    first_pack = jnp.concatenate(
        [to_blocks(grad_dec_mid, mid_rows), to_blocks(dec_in_wide, piece)], axis=3
    ).astype(BF)
    second_pack = jnp.concatenate(
        [to_blocks(grad_enc_mid, mid_rows), to_blocks(grad_heads, head_rows)], axis=3
    ).astype(BF)

    def scatter_all(pack):
        flat = pack.reshape((wide_count * row_split,) + pack.shape[2:])
        return lax.psum_scatter(flat, ALL, scatter_dimension=0, tiled=True)[0].astype(F32)

    first_sum = scatter_all(first_pack)
    second_sum = scatter_all(second_pack)
    in_pieces = lax.all_gather(first_sum[:, mid_rows:], ("pair", "chip"))
    dec_in_grad = in_pieces.transpose(0, 2, 1).reshape(row_split * piece, block_units)[:latent]

    wide_index = lax.axis_index("wide")
    per_row = 8 // row_split

    def mine_of(rows_full):
        stacked = jnp.stack(rows_full)
        return lax.dynamic_slice(
            stacked, (block_id * per_row, wide_index * block_units), (per_row, block_units)
        )

    norm_grad = mine_of(
        [gain_one, gain_two, gain_three, gain_four, shift_one, shift_two, shift_three, shift_four]
    )
    unbias = count_all / (count_all - 1.0)
    stats = mine_of(
        [
            centre_one,
            centre_two,
            centre_three,
            centre_four,
            spread_one * unbias,
            spread_two * unbias,
            spread_three * unbias,
            spread_four * unbias,
        ]
    )
    running_next = (1.0 - MOMENTUM) * running_stats + MOMENTUM * stats
    return (
        loss,
        input_grad,
        enc_in_grad.T,
        second_sum[:, :mid_rows].T,
        second_sum[:, mid_rows:].T,
        dec_in_grad,
        first_sum[:, :mid_rows].T,
        dec_out_grad.T,
        norm_grad,
        head_bias_grad,
        out_bias_grad,
        running_next,
    )


def solution(mesh):
    split = P(("pair", "chip"), "wide")
    by_cell = P(("wide", "pair", "chip"), None)
    return jax.shard_map(
        on_device,
        mesh=mesh,
        in_specs=(
            by_cell,
            by_cell,
            P(("wide", "pair", "chip")),
            P(),
            split,
            split,
            split,
            P(None, "wide"),
            split,
            split,
            split,
            P(),
            P(),
            split,
        ),
        out_specs=(
            P(),
            by_cell,
            split,
            split,
            split,
            P(None, "wide"),
            split,
            split,
            split,
            P(),
            P(),
            split,
        ),
        check_vma=False,
    )
```

time: 2060 us -> 726 us (0.35)
  waiting for transfers between devices: 872 us -> 239 us
  blocking collectives: 616 us -> 7.77 us
  local copies, waits for them, and re-layouts: 423 us -> 164 us
  starting transfers between devices: 0.28 us -> 125 us
  other arithmetic: 10.8 us -> 76.3 us
    unnamed x8 -> x4, waiting for transfers between devices: 712 us -> 10.1 us
    psum x12 -> x0, blocking collectives: 514 us -> none  [the longest x4 177 us: batch_moments(): lax.psum(jnp.sum(pre_act, axis=0), ('wide', 'pair', 'chip')) / count_all]
    reshape x20 -> x15, local copies, waits for them, and re-layouts: 245 us -> 29.7 us  [the longest x4 9.03 us: pick(): return part.transpose(0, 2, 1, 3).reshape(units, row_split * size)]
    all_gather x6 -> x1, waiting for transfers between devices: 160 us -> 0.02 us  [on_device(): mine = lax.all_gather(packed, ('wide', 'pair'))]
    ppermute x0 -> x84, waiting for transfers between devices: none -> 118 us  [the longest x64 107 us: swap_pair(): return lax.ppermute(value, 'pair', [(i, i ^ bits) for i in range(count)])]
    reduce_scatter x0 -> x1, waiting for transfers between devices: none -> 109 us  [scatter_all(): lax.psum_scatter(flat, ALL, scatter_dimension=0, tiled=True)[0].astype(F32)]
    all_gather x7 -> x1, blocking collectives: 102 us -> 7.77 us  [on_device(): in_pieces = lax.all_gather(first_sum[:, mid_rows:], ('pair', 'chip'))]
    ppermute x0 -> x84, starting transfers between devices: none -> 86.7 us  [the longest x64 69.2 us: swap_pair(): return lax.ppermute(value, 'pair', [(i, i ^ bits) for i in range(count)])]
  transfers between devices with their start and end apart: 7 -> 95, of which waited for: 4 -> 26; matrix products, arithmetic and copies ran while one was open for 3% -> 37% of each run, Pallas kernels for 0% -> 0%
where the time goes in v1:
time: 726 us; the launch traced here: 719 us
  waiting for transfers between devices  239 us (33%)
  local copies, waits for them, and re-layouts  164 us (23%)
  starting transfers between devices  125 us (17%)
  matrix products  85.1 us (12%)
  other arithmetic  76.3 us (11%)
  between operations  22.4 us (3%)
  blocking collectives  7.77 us (1%)
    reduce_scatter x1, waiting for transfers between devices, scatter_all(): lax.psum_scatter(flat, ALL, scatter_dimension=0, tiled=True)[0].astype(F32)  109 us
    ppermute x64, waiting for transfers between devices, swap_pair(): return lax.ppermute(value, 'pair', [(i, i ^ bits) for i in range(count)])  107 us
    dot_general x76, matrix products, dot(): lax.dot_general(left, right, (dims, ((), ())), preferred_element_type=F32)  85.1 us
    ppermute x64, starting transfers between devices, swap_pair(): return lax.ppermute(value, 'pair', [(i, i ^ bits) for i in range(count)])  69.2 us
    all_to_all x8, starting transfers between devices, share(): lax.all_to_all(jnp.broadcast_to(value[None], (count,) + value.shape), ALL...  38.2 us
    unnamed x330, local copies, waits for them, and re-layouts  31.4 us
    ppermute x12, starting transfers between devices, next_wide(): lax.ppermute(value, 'wide', [(i, (i + 1) % count) for i in range(count)])  16.5 us
  transfers between devices with their start and end apart: 95, of which 26 were waited for; matrix products, arithmetic and copies ran while one was open for 37% of the time, Pallas kernels for 0%

profile of v1, /device:TPU:0, one launch (start us, length us, event | category | flops | bytes accessed | tf_op | source)
XLA Modules:
  0.0 718.7 jit_solution(4456291566944415008)
XLA Ops:
  7.2 3.1 collective-permute-start.1
  10.3 4.9 reshape.502
  15.2 3.2 dynamic-slice_bitcast_fusion.1
  18.6 2.1 copy.121
  25.8 6.3 collective-permute-done.14
  47.4 5.1 collective-permute-done.16
  57.7 7.3 %collective-permute-done.19 = bf16[96,875]{1,0:T(8,128)(2,1)S(1)} collective-permute-done((bf16[96,875]{1,0:T(8,128)(2,1)S(1)}, bf16[96,875]{1,0:T(8,128)(2,1)S(1)}, u32[]{:S(2)}, u32[]{:S(2)}) %collective-permute-start.19) | collective-permute-done | bytes 168032 | tf_op jit(solution)/shard_map/ppermute | solution.py:33
  73.2 7.0 collective-permute-done.4
  80.2 2.3 collective-permute-start.7
  82.5 2.6 fusion.136
  92.2 2.1 collective-permute-start.31
  106.4 8.5 %collective-permute-done.8 = bf16[200,875]{1,0:T(8,128)(2,1)} collective-permute-done((bf16[200,875]{1,0:T(8,128)(2,1)S(1)}, bf16[200,875]{1,0:T(8,128)(2,1)}, u32[]{:S(2)}, u32[]{:S(2)}) %collective-permute-start.8) | collective-permute-done | bytes 350032 | tf_op jit(solution)/shard_map/ppermute | solution.py:42
  118.5 7.1 collective-permute-done.32
  130.2 2.6 all-to-all-start
  146.7 2.2 convert_bitcast_fusion
  148.9 2.5 slice_bitcast_fusion
  151.4 3.3 copy.135
  156.2 2.8 copy.132
  159.0 3.9 reshape.511
  164.6 2.2 fusion.140
  168.8 3.3 all-to-all-start.1
  180.1 2.0 copy.131
  187.6 5.9 all-to-all-start.2
  210.3 3.9 reshape.508
  218.7 6.0 all-to-all-start.3
  248.4 4.3 convert_reduce_fusion.2
  256.2 4.3 convert_reduce_fusion
  263.9 2.6 fusion.111
  266.5 4.3 convert_reduce_fusion.1
  280.8 4.4 convert_reduce_fusion.3
  290.2 2.4 add_add_fusion
  320.8 2.4 fusion.146
  332.3 2.4 broadcast_in_dim.56
  334.7 4.7 all-to-all-start.4
  345.9 9.3 %collective-permute-done.79 = bf16[96,875]{1,0:T(8,128)(2,1)S(1)} collective-permute-done((bf16[96,875]{1,0:T(8,128)(2,1)}, bf16[96,875]{1,0:T(8,128)(2,1)S(1)}, u32[]{:S(2)}, u32[]{:S(2)}) %collective-permute-start.79) | collective-permute-done | bytes 168032 | tf_op jit(solution)/shard_map/ppermute | solution.py:33
  366.1 16.4 %collective-permute-done.80 = bf16[200,875]{1,0:T(8,128)(2,1)S(1)} collective-permute-done((bf16[200,875]{1,0:T(8,128)(2,1)S(1)}, bf16[200,875]{1,0:T(8,128)(2,1)S(1)}, u32[]{:S(2)}, u32[]{:S(2)}) %collective-permute-start.80) | collective-permute-done | bytes 350032 | tf_op jit(solution)/shard_map/ppermute | solution.py:33
  388.9 2.0 fusion.132
  391.8 4.8 all-to-all-start.5
  399.9 2.1 add_convert_fusion.1
  404.1 2.9 reshape.522
  417.0 7.1 all-to-all-start.6
  426.1 3.5 pad_maximum_fusion.5
  434.3 2.3 add_convert_fusion
  441.7 2.0 fusion.130
  444.6 3.7 all-to-all-start.7
  449.9 2.4 add_bitcast_fusion
  458.8 2.8 multiply_convert_fusion.4
  462.4 2.0 reshape.520
  466.0 2.9 pad_maximum_fusion.1
  485.1 2.3 multiply_subtract_fusion.2
  493.0 2.4 multiply_subtract_fusion.3
  495.7 2.1 copy.146
  500.5 4.3 collective-permute-done.56
  505.1 5.8 collective-permute-done.60
  512.1 10.1 %collective-permute-done.61 = bf16[200,875]{1,0:T(8,128)(2,1)S(1)} collective-permute-done((bf16[200,875]{1,0:T(8,128)(2,1)S(1)}, bf16[200,875]{1,0:T(8,128)(2,1)S(1)}, u32[]{:S(2)}, u32[]{:S(2)}) %collective-permute-start.61) | collective-permute-done | bytes 350032 | tf_op jit(solution)/shard_map/ppermute | solution.py:33
  525.5 7.4 %collective-permute-done.57 = bf16[200,875]{1,0:T(8,128)(2,1)S(1)} collective-permute-done((bf16[200,875]{1,0:T(8,128)(2,1)S(1)}, bf16[200,875]{1,0:T(8,128)(2,1)S(1)}, u32[]{:S(2)}, u32[]{:S(2)}) %collective-permute-start.57) | collective-permute-done | bytes 350032 | tf_op jit(solution)/shard_map/ppermute | solution.py:33
  538.1 12.9 %collective-permute-done.53 = bf16[200,875]{1,0:T(8,128)(2,1)S(1)} collective-permute-done((bf16[200,875]{1,0:T(8,128)(2,1)S(1)}, bf16[200,875]{1,0:T(8,128)(2,1)S(1)}, u32[]{:S(2)}, u32[]{:S(2)}) %collective-permute-start.53) | collective-permute-done | bytes 350032 | tf_op jit(solution)/shard_map/ppermute | solution.py:33
  552.9 3.5 broadcast_in_dim.57
  557.5 3.0 collective-permute-done.47
  562.5 10.0 %reduce-scatter.8.cloned.1.call-done = bf16[1,200,113]{2,1,0:T(8,128)(2,1)} async-done(((bf16[32,200,113]{2,1,0:T(8,128)(2,1)}), bf16[1,200,113]{2,1,0:T(8,128)(2,1)}) %reduce-scatter.8.cloned.1.call-update) | async-done | bytes 45216
  573.5 7.8 %all-gather.2 = f32[8,200,13]{1,2,0:T(8,128)S(1)} all-gather(f32[1,200,13]{1,2,0:T(8,128)S(1)} %copy.155), channel_id=3, replica_groups=mesh['wide'=4,'pair'=4,'chip'=2] {'pair','chip'}, dimensions={0}, use_global_device_ids=true | all-gather | bytes 93600 | tf_op jit(solution)/shard_map/all_gather | solution.py:375
  582.7 2.6 fusion.135
  592.4 7.0 reshape.519
  599.3 109.0 %reduce-scatter.6.cloned.1.call-done = bf16[1,200,125]{1,2,0:T(8,128)(2,1)} async-done(((bf16[32,200,125]{1,2,0:T(8,128)(2,1)}), bf16[1,200,125]{1,2,0:T(8,128)(2,1)}) %reduce-scatter.6.cloned.1.call-update) | async-done | bytes 50016 | tf_op jit(solution)/shard_map/reduce_scatter | solution.py:371
  (814 shorter events, 305.4 us)
Async XLA Ops:
  7.2 121.8 %all-gather.5.cloned.1.call-start = ((), (), s32[]{:S(2)}) async-start(), calls=%async_computation.11 | async-start | bytes 1740800 | tf_op jit(solution)/shard_map/all_gather | solution.py:184
  7.2 16.5 %collective-permute-start.1 = (bf16[200,875]{1,0:T(8,128)(2,1)}, bf16[200,875]{1,0:T(8,128)(2,1)}, u32[]{:S(2)}, u32[]{:S(2)}) collective-permute-start(bf16[200,875]{1,0:T(8,128)(2,1)} %bitcast.8), channel_id=1, source_target_pairs={{0,8},{8,16},{16,24},{24,0},{1,9},{9,17},{17,25},{25,1},{2,10},{10... | collective-permute-start | bytes 1050008 | tf_op jit(solution)/shard_map/ppermute | solution.py:42
  20.7 61.8 %collective-permute-start = (bf16[4,875,256]{2,0,1:T(4,128)(2,1)}, bf16[4,875,256]{2,0,1:T(4,128)(2,1)S(1)}, u32[]{:S(2)}, u32[]{:S(2)}) collective-permute-start(bf16[4,875,256]{2,0,1:T(4,128)(2,1)} %copy.121), channel_id=1, source_target_pairs={{0,1},{1,0},{2,3},{3,2},{4,5},{5,4},{6,7},{7,6},{8,9},{9,8},{10,11... | collective-permute-start | bytes 5376008 | tf_op jit(solution)/shard_map/ppermute | solution.py:37
  23.8 14.6 %collective-permute-start.2 = (bf16[200,875]{1,0:T(8,128)(2,1)}, bf16[200,875]{1,0:T(8,128)(2,1)}, u32[]{:S(2)}, u32[]{:S(2)}) collective-permute-start(bf16[200,875]{1,0:T(8,128)(2,1)} %collective-permute-done.1), channel_id=1, source_target_pairs={{0,8},{8,16},{16,24},{24,0},{1,9},{9,17},{17,25},{25,1},{2,10},{10... | collective-permute-start | bytes 1050008 | tf_op jit(solution)/shard_map/ppermute | solution.py:42
  25.3 19.2 %collective-permute-start.18 = (bf16[200,875]{1,0:T(8,128)(2,1)}, bf16[200,875]{1,0:T(8,128)(2,1)S(1)}, u32[]{:S(2)}, u32[]{:S(2)}) collective-permute-start(bf16[200,875]{1,0:T(8,128)(2,1)} %collective-permute-done.1), channel_id=1, source_target_pairs={{0,4},{2,6},{4,0},{6,2},{1,5},{3,7},{5,1},{7,3},{8,12},{10,14},{12... | collective-permute-start | bytes 1050008 | tf_op jit(solution)/shard_map/ppermute | solution.py:33
  35.1 19.0 %collective-permute-start.17 = (bf16[200,875]{1,0:T(8,128)(2,1)}, bf16[200,875]{1,0:T(8,128)(2,1)}, u32[]{:S(2)}, u32[]{:S(2)}) collective-permute-start(bf16[200,875]{1,0:T(8,128)(2,1)} %collective-permute-done.1), channel_id=1, source_target_pairs={{0,2},{2,0},{4,6},{6,4},{1,3},{3,1},{5,7},{7,5},{8,10},{10,8},{12,... | collective-permute-start | bytes 1050008 | tf_op jit(solution)/shard_map/ppermute | solution.py:33
  38.4 17.1 %collective-permute-start.22 = (bf16[200,875]{1,0:T(8,128)(2,1)}, bf16[200,875]{1,0:T(8,128)(2,1)S(1)}, u32[]{:S(2)}, u32[]{:S(2)}) collective-permute-start(bf16[200,875]{1,0:T(8,128)(2,1)} %collective-permute-done.2), channel_id=1, source_target_pairs={{0,4},{2,6},{4,0},{6,2},{1,5},{3,7},{5,1},{7,3},{8,12},{10,14},{12... | collective-permute-start | bytes 1050008 | tf_op jit(solution)/shard_map/ppermute | solution.py:33
  40.4 16.8 %collective-permute-start.3 = (bf16[200,875]{1,0:T(8,128)(2,1)}, bf16[200,875]{1,0:T(8,128)(2,1)}, u32[]{:S(2)}, u32[]{:S(2)}) collective-permute-start(bf16[200,875]{1,0:T(8,128)(2,1)} %collective-permute-done.2), channel_id=1, source_target_pairs={{0,8},{8,16},{16,24},{24,0},{1,9},{9,17},{17,25},{25,1},{2,10},{10... | collective-permute-start | bytes 1050008 | tf_op jit(solution)/shard_map/ppermute | solution.py:42
  52.6 14.0 %collective-permute-start.21 = (bf16[200,875]{1,0:T(8,128)(2,1)}, bf16[200,875]{1,0:T(8,128)(2,1)S(1)}, u32[]{:S(2)}, u32[]{:S(2)}) collective-permute-start(bf16[200,875]{1,0:T(8,128)(2,1)} %collective-permute-done.2), channel_id=1, source_target_pairs={{0,2},{2,0},{4,6},{6,4},{1,3},{3,1},{5,7},{7,5},{8,10},{10,8},{12,... | collective-permute-start | bytes 1050008 | tf_op jit(solution)/shard_map/ppermute | solution.py:33
  57.2 13.3 %collective-permute-start.5 = (bf16[200,875]{1,0:T(8,128)(2,1)}, bf16[200,875]{1,0:T(8,128)(2,1)S(1)}, u32[]{:S(2)}, u32[]{:S(2)}) collective-permute-start(bf16[200,875]{1,0:T(8,128)(2,1)} %collective-permute-done.3), channel_id=1, source_target_pairs={{0,4},{2,6},{4,0},{6,2},{1,5},{3,7},{5,1},{7,3},{8,12},{10,14},{12... | collective-permute-start | bytes 1050008 | tf_op jit(solution)/shard_map/ppermute | solution.py:33
  91.2 13.3 %collective-permute-start.27 = (bf16[200,875]{1,0:T(8,128)(2,1)S(1)}, bf16[200,875]{1,0:T(8,128)(2,1)S(1)}, u32[]{:S(2)}, u32[]{:S(2)}) collective-permute-start(bf16[200,875]{1,0:T(8,128)(2,1)S(1)} %bitcast.346), channel_id=1, source_target_pairs={{0,2},{2,0},{4,6},{6,4},{1,3},{3,1},{5,7},{7,5},{8,10},{10,8},{12,... | collective-permute-start | bytes 1050008 | tf_op jit(solution)/shard_map/ppermute | solution.py:33
  102.0 26.5 %collective-permute-start.25 = (f32[800,256]{1,0:T(8,128)S(1)}, f32[800,256]{1,0:T(8,128)S(1)}, u32[]{:S(2)}, u32[]{:S(2)}) collective-permute-start(f32[800,256]{1,0:T(8,128)S(1)} %slice.550), channel_id=1, source_target_pairs={{0,1},{1,0},{2,3},{3,2},{4,5},{5,4},{6,7},{7,6},{8,9},{9,8},{10,11... | collective-permute-start | bytes 2457608 | tf_op jit(solution)/shard_map/ppermute | solution.py:37
  103.8 13.0 %collective-permute-start.35 = (bf16[96,875]{1,0:T(8,128)(2,1)S(1)}, bf16[96,875]{1,0:T(8,128)(2,1)S(1)}, u32[]{:S(2)}, u32[]{:S(2)}) collective-permute-start(bf16[96,875]{1,0:T(8,128)(2,1)S(1)} %slice.570), channel_id=1, source_target_pairs={{0,2},{2,0},{4,6},{6,4},{1,3},{3,1},{5,7},{7,5},{8,10},{10,8},{12,... | collective-permute-start | bytes 504008 | tf_op jit(solution)/shard_map/ppermute | solution.py:33
  104.6 13.2 %collective-permute-start.36 = (bf16[104,875]{1,0:T(8,128)(2,1)S(1)}, bf16[104,875]{1,0:T(8,128)(2,1)S(1)}, u32[]{:S(2)}, u32[]{:S(2)}) collective-permute-start(bf16[104,875]{1,0:T(8,128)(2,1)S(1)} %slice.571), channel_id=1, source_target_pairs={{0,4},{2,6},{4,0},{6,2},{1,5},{3,7},{5,1},{7,3},{8,12},{10,14},{12... | collective-permute-start | bytes 546008 | tf_op jit(solution)/shard_map/ppermute | solution.py:33
  116.9 131.4 %collective-permute-start.11 = (bf16[8,256]{1,0:T(8,128)(2,1)}, bf16[8,256]{1,0:T(8,128)(2,1)}, u32[]{:S(2)}, u32[]{:S(2)}) collective-permute-start(bf16[8,256]{1,0:T(8,128)(2,1)} %fusion.93), channel_id=1, source_target_pairs={{0,1},{1,0},{2,3},{3,2},{4,5},{5,4},{6,7},{7,6},{8,9},{9,8},{10,11... | collective-permute-start | bytes 12296 | tf_op jit(solution)/shard_map/ppermute | solution.py:37
  117.8 15.8 %collective-permute-start.9 = (bf16[200,875]{1,0:T(8,128)(2,1)}, bf16[200,875]{1,0:T(8,128)(2,1)}, u32[]{:S(2)}, u32[]{:S(2)}) collective-permute-start(bf16[200,875]{1,0:T(8,128)(2,1)} %collective-permute-done.8), channel_id=1, source_target_pairs={{0,8},{8,16},{16,24},{24,0},{1,9},{9,17},{17,25},{25,1},{2,10},{10... | collective-permute-start | bytes 1050008 | tf_op jit(solution)/shard_map/ppermute | solution.py:42
  128.1 65.4 %collective-permute-start.38 = (bf16[104,875]{1,0:T(8,128)(2,1)}, bf16[104,875]{1,0:T(8,128)(2,1)}, u32[]{:S(2)}, u32[]{:S(2)}) collective-permute-start(bf16[104,875]{1,0:T(8,128)(2,1)} %slice.573), channel_id=1, source_target_pairs={{0,4},{2,6},{4,0},{6,2},{1,5},{3,7},{5,1},{7,3},{8,12},{10,14},{12... | collective-permute-start | bytes 546008 | tf_op jit(solution)/shard_map/ppermute | solution.py:33
  129.0 14.5 %collective-permute-start.12 = (bf16[16,200,239]{2,1,0:T(8,128)(2,1)}, bf16[16,200,239]{2,1,0:T(8,128)(2,1)}, u32[]{:S(2)}, u32[]{:S(2)}) collective-permute-start(bf16[16,200,239]{2,1,0:T(8,128)(2,1)} %bitcast.323), channel_id=1, source_target_pairs={{0,1},{1,0},{2,3},{3,2},{4,5},{5,4},{6,7},{7,6},{8,9},{9,8},{10,11... | collective-permute-start | bytes 4588808 | tf_op jit(solution)/shard_map/ppermute | solution.py:37
  133.6 64.8 %collective-permute-start.29 = (bf16[200,875]{1,0:T(8,128)(2,1)}, bf16[200,875]{1,0:T(8,128)(2,1)}, u32[]{:S(2)}, u32[]{:S(2)}) collective-permute-start(bf16[200,875]{1,0:T(8,128)(2,1)} %collective-permute-done.9), channel_id=1, source_target_pairs={{0,2},{2,0},{4,6},{6,4},{1,3},{3,1},{5,7},{7,5},{8,10},{10,8},{12,... | collective-permute-start | bytes 1050008 | tf_op jit(solution)/shard_map/ppermute | solution.py:33
  137.9 63.6 %collective-permute-start.10 = (bf16[200,875]{1,0:T(8,128)(2,1)}, bf16[200,875]{1,0:T(8,128)(2,1)}, u32[]{:S(2)}, u32[]{:S(2)}) collective-permute-start(bf16[200,875]{1,0:T(8,128)(2,1)} %collective-permute-done.9), channel_id=1, source_target_pairs={{0,8},{8,16},{16,24},{24,0},{1,9},{9,17},{17,25},{25,1},{2,10},{10... | collective-permute-start | bytes 1050008 | tf_op jit(solution)/shard_map/ppermute | solution.py:42
  143.5 51.6 %collective-permute-start.33 = (bf16[200,875]{1,0:T(8,128)(2,1)}, bf16[200,875]{1,0:T(8,128)(2,1)}, u32[]{:S(2)}, u32[]{:S(2)}) collective-permute-start(bf16[200,875]{1,0:T(8,128)(2,1)} %collective-permute-done.9), channel_id=1, source_target_pairs={{0,4},{2,6},{4,0},{6,2},{1,5},{3,7},{5,1},{7,3},{8,12},{10,14},{12... | collective-permute-start | bytes 1050008 | tf_op jit(solution)/shard_map/ppermute | solution.py:33
  168.8 13.6 %all-to-all-start.1 = ((f32[32,2,800]{2,1,0:T(2,128)}), f32[32,2,800]{2,1,0:T(2,128)}, u32[]{:S(2)}, u32[]{:S(2)}) async-start(f32[32,2,800]{2,1,0:T(2,128)} %broadcast_in_dim.46), calls=%async_computation.1 | async-start | bytes 458752 | tf_op jit(solution)/shard_map/all_to_all | solution.py:108
  187.6 26.6 %all-to-all-start.2 = ((f32[32,2,800]{2,1,0:T(2,128)}), f32[32,2,800]{2,1,0:T(2,128)}, u32[]{:S(2)}, u32[]{:S(2)}) async-start(f32[32,2,800]{2,1,0:T(2,128)} %broadcast_in_dim.47), calls=%async_computation.2 | async-start | bytes 458752 | tf_op jit(solution)/shard_map/all_to_all | solution.py:108
  196.7 27.9 %collective-permute-start.39 = (bf16[96,875]{1,0:T(8,128)(2,1)}, bf16[96,875]{1,0:T(8,128)(2,1)}, u32[]{:S(2)}, u32[]{:S(2)}) collective-permute-start(bf16[96,875]{1,0:T(8,128)(2,1)} %slice.574), channel_id=1, source_target_pairs={{0,2},{2,0},{4,6},{6,4},{1,3},{3,1},{5,7},{7,5},{8,10},{10,8},{12,... | collective-permute-start | bytes 504008 | tf_op jit(solution)/shard_map/ppermute | solution.py:33
  200.1 26.2 %collective-permute-start.40 = (bf16[104,875]{1,0:T(8,128)(2,1)}, bf16[104,875]{1,0:T(8,128)(2,1)S(1)}, u32[]{:S(2)}, u32[]{:S(2)}) collective-permute-start(bf16[104,875]{1,0:T(8,128)(2,1)} %slice.575), channel_id=1, source_target_pairs={{0,4},{2,6},{4,0},{6,2},{1,5},{3,7},{5,1},{7,3},{8,12},{10,14},{12... | collective-permute-start | bytes 546008 | tf_op jit(solution)/shard_map/ppermute | solution.py:33
  201.5 28.8 %collective-permute-start.30 = (bf16[200,875]{1,0:T(8,128)(2,1)}, bf16[200,875]{1,0:T(8,128)(2,1)}, u32[]{:S(2)}, u32[]{:S(2)}) collective-permute-start(bf16[200,875]{1,0:T(8,128)(2,1)} %collective-permute-done.10), channel_id=1, source_target_pairs={{0,2},{2,0},{4,6},{6,4},{1,3},{3,1},{5,7},{7,5},{8,10},{10,8},{12,... | collective-permute-start | bytes 1050008 | tf_op jit(solution)/shard_map/ppermute | solution.py:33
  202.1 24.9 %collective-permute-start.34 = (bf16[200,875]{1,0:T(8,128)(2,1)}, bf16[200,875]{1,0:T(8,128)(2,1)}, u32[]{:S(2)}, u32[]{:S(2)}) collective-permute-start(bf16[200,875]{1,0:T(8,128)(2,1)} %collective-permute-done.10), channel_id=1, source_target_pairs={{0,4},{2,6},{4,0},{6,2},{1,5},{3,7},{5,1},{7,3},{8,12},{10,14},{12... | collective-permute-start | bytes 1050008 | tf_op jit(solution)/shard_map/ppermute | solution.py:33
  218.7 18.3 %all-to-all-start.3 = ((f32[32,2,800]{2,1,0:T(2,128)}), f32[32,2,800]{2,1,0:T(2,128)S(1)}, u32[]{:S(2)}, u32[]{:S(2)}) async-start(f32[32,2,800]{2,1,0:T(2,128)} %broadcast_in_dim.48), calls=%async_computation.3 | async-start | bytes 458752 | tf_op jit(solution)/shard_map/all_to_all | solution.py:108
  293.7 33.8 %collective-permute-start.43 = (f32[800,256]{1,0:T(8,128)}, f32[800,256]{1,0:T(8,128)}, u32[]{:S(2)}, u32[]{:S(2)}) collective-permute-start(f32[800,256]{1,0:T(8,128)} %slice.579), channel_id=1, source_target_pairs={{0,1},{1,0},{2,3},{3,2},{4,5},{5,4},{6,7},{7,6},{8,9},{9,8},{10,11... | collective-permute-start | bytes 2457608 | tf_op jit(solution)/shard_map/ppermute | solution.py:37
  300.7 129.0 %collective-permute-start.65 = (bf16[104,875]{1,0:T(8,128)(2,1)}, bf16[104,875]{1,0:T(8,128)(2,1)}, u32[]{:S(2)}, u32[]{:S(2)}) collective-permute-start(bf16[104,875]{1,0:T(8,128)(2,1)} %slice.632), channel_id=1, source_target_pairs={{0,4},{2,6},{4,0},{6,2},{1,5},{3,7},{5,1},{7,3},{8,12},{10,14},{12... | collective-permute-start | bytes 546008 | tf_op jit(solution)/shard_map/ppermute | solution.py:33
  303.0 20.2 %collective-permute-start.67 = (bf16[96,875]{1,0:T(8,128)(2,1)}, bf16[96,875]{1,0:T(8,128)(2,1)}, u32[]{:S(2)}, u32[]{:S(2)}) collective-permute-start(bf16[96,875]{1,0:T(8,128)(2,1)} %slice.634), channel_id=1, source_target_pairs={{0,2},{2,0},{4,6},{6,4},{1,3},{3,1},{5,7},{7,5},{8,10},{10,8},{12,... | collective-permute-start | bytes 504008 | tf_op jit(solution)/shard_map/ppermute | solution.py:33
  304.9 53.6 %collective-permute-start.69 = (bf16[104,875]{1,0:T(8,128)(2,1)}, bf16[104,875]{1,0:T(8,128)(2,1)}, u32[]{:S(2)}, u32[]{:S(2)}) collective-permute-start(bf16[104,875]{1,0:T(8,128)(2,1)} %slice.638), channel_id=1, source_target_pairs={{0,4},{2,6},{4,0},{6,2},{1,5},{3,7},{5,1},{7,3},{8,12},{10,14},{12... | collective-permute-start | bytes 546008 | tf_op jit(solution)/shard_map/ppermute | solution.py:33
  308.4 17.1 %collective-permute-start.71 = (bf16[96,875]{1,0:T(8,128)(2,1)}, bf16[96,875]{1,0:T(8,128)(2,1)}, u32[]{:S(2)}, u32[]{:S(2)}) collective-permute-start(bf16[96,875]{1,0:T(8,128)(2,1)} %slice.640), channel_id=1, source_target_pairs={{0,2},{2,0},{4,6},{6,4},{1,3},{3,1},{5,7},{7,5},{8,10},{10,8},{12,... | collective-permute-start | bytes 504008 | tf_op jit(solution)/shard_map/ppermute | solution.py:33
  323.2 40.3 %collective-permute-start.73 = (bf16[104,875]{1,0:T(8,128)(2,1)}, bf16[104,875]{1,0:T(8,128)(2,1)}, u32[]{:S(2)}, u32[]{:S(2)}) collective-permute-start(bf16[104,875]{1,0:T(8,128)(2,1)} %slice.644), channel_id=1, source_target_pairs={{0,4},{2,6},{4,0},{6,2},{1,5},{3,7},{5,1},{7,3},{8,12},{10,14},{12... | collective-permute-start | bytes 546008 | tf_op jit(solution)/shard_map/ppermute | solution.py:33
  325.5 13.9 %collective-permute-start.75 = (bf16[96,875]{1,0:T(8,128)(2,1)}, bf16[96,875]{1,0:T(8,128)(2,1)}, u32[]{:S(2)}, u32[]{:S(2)}) collective-permute-start(bf16[96,875]{1,0:T(8,128)(2,1)} %slice.646), channel_id=1, source_target_pairs={{0,2},{2,0},{4,6},{6,4},{1,3},{3,1},{5,7},{7,5},{8,10},{10,8},{12,... | collective-permute-start | bytes 504008 | tf_op jit(solution)/shard_map/ppermute | solution.py:33
  327.5 32.6 %collective-permute-start.77 = (bf16[104,875]{1,0:T(8,128)(2,1)}, bf16[104,875]{1,0:T(8,128)(2,1)}, u32[]{:S(2)}, u32[]{:S(2)}) collective-permute-start(bf16[104,875]{1,0:T(8,128)(2,1)} %slice.650), channel_id=1, source_target_pairs={{0,4},{2,6},{4,0},{6,2},{1,5},{3,7},{5,1},{7,3},{8,12},{10,14},{12... | collective-permute-start | bytes 546008 | tf_op jit(solution)/shard_map/ppermute | solution.py:33
  334.7 51.0 %all-to-all-start.4 = ((f32[32,1,8601]{2,1,0:T(1,128)}), f32[32,1,8601]{2,1,0:T(1,128)}, u32[]{:S(2)}, u32[]{:S(2)}) async-start(f32[32,1,8601]{2,1,0:T(1,128)} %broadcast_in_dim.56), calls=%async_computation.4 | async-start | bytes 2228224 | tf_op jit(solution)/shard_map/all_to_all | solution.py:108
  339.4 15.7 %collective-permute-start.79 = (bf16[96,875]{1,0:T(8,128)(2,1)}, bf16[96,875]{1,0:T(8,128)(2,1)S(1)}, u32[]{:S(2)}, u32[]{:S(2)}) collective-permute-start(bf16[96,875]{1,0:T(8,128)(2,1)} %slice.652), channel_id=1, source_target_pairs={{0,2},{2,0},{4,6},{6,4},{1,3},{3,1},{5,7},{7,5},{8,10},{10,8},{12,... | collective-permute-start | bytes 504008 | tf_op jit(solution)/shard_map/ppermute | solution.py:33
  355.2 93.2 %collective-permute-start.68 = (bf16[200,875]{1,0:T(8,128)(2,1)}, bf16[200,875]{1,0:T(8,128)(2,1)}, u32[]{:S(2)}, u32[]{:S(2)}) collective-permute-start(bf16[200,875]{1,0:T(8,128)(2,1)} %pad_maximum_fusion.24), channel_id=1, source_target_pairs={{0,4},{2,6},{4,0},{6,2},{1,5},{3,7},{5,1},{7,3},{8,12},{10,14},{12... | collective-permute-start | bytes 1050008 | tf_op jit(solution)/shard_map/ppermute | solution.py:33
  358.6 38.1 %collective-permute-start.76 = (bf16[200,875]{1,0:T(8,128)(2,1)}, bf16[200,875]{1,0:T(8,128)(2,1)}, u32[]{:S(2)}, u32[]{:S(2)}) collective-permute-start(bf16[200,875]{1,0:T(8,128)(2,1)} %pad_maximum_fusion.28), channel_id=1, source_target_pairs={{0,4},{2,6},{4,0},{6,2},{1,5},{3,7},{5,1},{7,3},{8,12},{10,14},{12... | collective-permute-start | bytes 1050008 | tf_op jit(solution)/shard_map/ppermute | solution.py:33
  360.1 22.4 %collective-permute-start.80 = (bf16[200,875]{1,0:T(8,128)(2,1)S(1)}, bf16[200,875]{1,0:T(8,128)(2,1)S(1)}, u32[]{:S(2)}, u32[]{:S(2)}) collective-permute-start(bf16[200,875]{1,0:T(8,128)(2,1)S(1)} %pad_maximum_fusion.30), channel_id=1, source_target_pairs={{0,4},{2,6},{4,0},{6,2},{1,5},{3,7},{5,1},{7,3},{8,12},{10,14},{12... | collective-permute-start | bytes 1050008 | tf_op jit(solution)/shard_map/ppermute | solution.py:33
  363.5 20.0 %collective-permute-start.78 = (bf16[200,875]{1,0:T(8,128)(2,1)S(1)}, bf16[200,875]{1,0:T(8,128)(2,1)S(1)}, u32[]{:S(2)}, u32[]{:S(2)}) collective-permute-start(bf16[200,875]{1,0:T(8,128)(2,1)S(1)} %pad_maximum_fusion.29), channel_id=1, source_target_pairs={{0,2},{2,0},{4,6},{6,4},{1,3},{3,1},{5,7},{7,5},{8,10},{10,8},{12,... | collective-permute-start | bytes 1050008 | tf_op jit(solution)/shard_map/ppermute | solution.py:33
  382.6 15.8 %collective-permute-start.74 = (bf16[200,875]{1,0:T(8,128)(2,1)}, bf16[200,875]{1,0:T(8,128)(2,1)}, u32[]{:S(2)}, u32[]{:S(2)}) collective-permute-start(bf16[200,875]{1,0:T(8,128)(2,1)} %pad_maximum_fusion.27), channel_id=1, source_target_pairs={{0,2},{2,0},{4,6},{6,4},{1,3},{3,1},{5,7},{7,5},{8,10},{10,8},{12,... | collective-permute-start | bytes 1050008 | tf_op jit(solution)/shard_map/ppermute | solution.py:33
  384.4 15.4 %collective-permute-start.81 = (bf16[200,875]{1,0:T(8,128)(2,1)}, bf16[200,875]{1,0:T(8,128)(2,1)}, u32[]{:S(2)}, u32[]{:S(2)}) collective-permute-start(bf16[200,875]{1,0:T(8,128)(2,1)} %add_convert_fusion.2), channel_id=1, source_target_pairs={{0,8},{8,16},{16,24},{24,0},{1,9},{9,17},{17,25},{25,1},{2,10},{10... | collective-permute-start | bytes 1050008 | tf_op jit(solution)/shard_map/ppermute | solution.py:42
  391.8 16.9 %all-to-all-start.5 = ((f32[32,2,800]{2,1,0:T(2,128)}), f32[32,2,800]{2,1,0:T(2,128)}, u32[]{:S(2)}, u32[]{:S(2)}) async-start(f32[32,2,800]{2,1,0:T(2,128)} %broadcast_in_dim.58), calls=%async_computation.5 | async-start | bytes 458752 | tf_op jit(solution)/shard_map/all_to_all | solution.py:108
  396.6 37.7 %collective-permute-start.72 = (bf16[200,875]{1,0:T(8,128)(2,1)}, bf16[200,875]{1,0:T(8,128)(2,1)}, u32[]{:S(2)}, u32[]{:S(2)}) collective-permute-start(bf16[200,875]{1,0:T(8,128)(2,1)} %pad_maximum_fusion.26), channel_id=1, source_target_pairs={{0,4},{2,6},{4,0},{6,2},{1,5},{3,7},{5,1},{7,3},{8,12},{10,14},{12... | collective-permute-start | bytes 1050008 | tf_op jit(solution)/shard_map/ppermute | solution.py:33
  398.4 35.9 %collective-permute-start.70 = (bf16[200,875]{1,0:T(8,128)(2,1)}, bf16[200,875]{1,0:T(8,128)(2,1)}, u32[]{:S(2)}, u32[]{:S(2)}) collective-permute-start(bf16[200,875]{1,0:T(8,128)(2,1)} %pad_maximum_fusion.25), channel_id=1, source_target_pairs={{0,2},{2,0},{4,6},{6,4},{1,3},{3,1},{5,7},{7,5},{8,10},{10,8},{12,... | collective-permute-start | bytes 1050008 | tf_op jit(solution)/shard_map/ppermute | solution.py:33
  402.0 32.4 %collective-permute-start.82 = (bf16[200,875]{1,0:T(8,128)(2,1)}, bf16[200,875]{1,0:T(8,128)(2,1)}, u32[]{:S(2)}, u32[]{:S(2)}) collective-permute-start(bf16[200,875]{1,0:T(8,128)(2,1)} %add_convert_fusion.1), channel_id=1, source_target_pairs={{0,8},{8,16},{16,24},{24,0},{1,9},{9,17},{17,25},{25,1},{2,10},{10... | collective-permute-start | bytes 1050008 | tf_op jit(solution)/shard_map/ppermute | solution.py:42
  417.0 21.1 %all-to-all-start.6 = ((f32[32,1,1800]{2,1,0:T(1,128)}), f32[32,1,1800]{2,1,0:T(1,128)}, u32[]{:S(2)}, u32[]{:S(2)}) async-start(f32[32,1,1800]{2,1,0:T(1,128)} %broadcast_in_dim.59), calls=%async_computation.6 | async-start | bytes 491520 | tf_op jit(solution)/shard_map/all_to_all | solution.py:108
  424.1 148.4 %reduce-scatter.8.cloned.1.call-start = ((), (), s32[]{:S(2)}) async-start(), calls=%async_computation.12 | async-start | bytes 1689600
  432.6 15.8 %collective-permute-start.66 = (bf16[200,875]{1,0:T(8,128)(2,1)}, bf16[200,875]{1,0:T(8,128)(2,1)}, u32[]{:S(2)}, u32[]{:S(2)}) collective-permute-start(bf16[200,875]{1,0:T(8,128)(2,1)} %pad_maximum_fusion.23), channel_id=1, source_target_pairs={{0,2},{2,0},{4,6},{6,4},{1,3},{3,1},{5,7},{7,5},{8,10},{10,8},{12,... | collective-permute-start | bytes 1050008 | tf_op jit(solution)/shard_map/ppermute | solution.py:33
  436.7 13.2 %collective-permute-start.83 = (bf16[200,875]{1,0:T(8,128)(2,1)}, bf16[200,875]{1,0:T(8,128)(2,1)}, u32[]{:S(2)}, u32[]{:S(2)}) collective-permute-start(bf16[200,875]{1,0:T(8,128)(2,1)} %add_convert_fusion), channel_id=1, source_target_pairs={{0,8},{8,16},{16,24},{24,0},{1,9},{9,17},{17,25},{25,1},{2,10},{10... | collective-permute-start | bytes 1050008 | tf_op jit(solution)/shard_map/ppermute | solution.py:42
  444.6 13.6 %all-to-all-start.7 = ((f32[32,2,800]{2,1,0:T(2,128)}), f32[32,2,800]{2,1,0:T(2,128)S(1)}, u32[]{:S(2)}, u32[]{:S(2)}) async-start(f32[32,2,800]{2,1,0:T(2,128)} %broadcast_in_dim.60), calls=%async_computation.7 | async-start | bytes 458752 | tf_op jit(solution)/shard_map/all_to_all | solution.py:108
  448.3 260.0 %reduce-scatter.6.cloned.1.call-start = ((), (), s32[]{:S(2)}) async-start(), calls=%async_computation.10 | async-start | bytes 2162688 | tf_op jit(solution)/shard_map/reduce_scatter | solution.py:371
  479.6 57.9 %collective-permute-start.46 = (bf16[104,875]{1,0:T(8,128)(2,1)S(1)}, bf16[104,875]{1,0:T(8,128)(2,1)S(1)}, u32[]{:S(2)}, u32[]{:S(2)}) collective-permute-start(bf16[104,875]{1,0:T(8,128)(2,1)S(1)} %slice.603), channel_id=1, source_target_pairs={{0,4},{2,6},{4,0},{6,2},{1,5},{3,7},{5,1},{7,3},{8,12},{10,14},{12... | collective-permute-start | bytes 546008 | tf_op jit(solution)/shard_map/ppermute | solution.py:33
  480.5 17.8 %collective-permute-start.48 = (bf16[96,875]{1,0:T(8,128)(2,1)S(1)}, bf16[96,875]{1,0:T(8,128)(2,1)S(1)}, u32[]{:S(2)}, u32[]{:S(2)}) collective-permute-start(bf16[96,875]{1,0:T(8,128)(2,1)S(1)} %slice.605), channel_id=1, source_target_pairs={{0,2},{2,0},{4,6},{6,4},{1,3},{3,1},{5,7},{7,5},{8,10},{10,8},{12,... | collective-permute-start | bytes 504008 | tf_op jit(solution)/shard_map/ppermute | solution.py:33
  481.4 42.8 %collective-permute-start.50 = (bf16[104,875]{1,0:T(8,128)(2,1)S(1)}, bf16[104,875]{1,0:T(8,128)(2,1)S(1)}, u32[]{:S(2)}, u32[]{:S(2)}) collective-permute-start(bf16[104,875]{1,0:T(8,128)(2,1)S(1)} %slice.609), channel_id=1, source_target_pairs={{0,4},{2,6},{4,0},{6,2},{1,5},{3,7},{5,1},{7,3},{8,12},{10,14},{12... | collective-permute-start | bytes 546008 | tf_op jit(solution)/shard_map/ppermute | solution.py:33
  482.6 16.6 %collective-permute-start.52 = (bf16[96,875]{1,0:T(8,128)(2,1)S(1)}, bf16[96,875]{1,0:T(8,128)(2,1)S(1)}, u32[]{:S(2)}, u32[]{:S(2)}) collective-permute-start(bf16[96,875]{1,0:T(8,128)(2,1)S(1)} %slice.611), channel_id=1, source_target_pairs={{0,2},{2,0},{4,6},{6,4},{1,3},{3,1},{5,7},{7,5},{8,10},{10,8},{12,... | collective-permute-start | bytes 504008 | tf_op jit(solution)/shard_map/ppermute | solution.py:33
  484.0 27.9 %collective-permute-start.54 = (bf16[104,875]{1,0:T(8,128)(2,1)S(1)}, bf16[104,875]{1,0:T(8,128)(2,1)S(1)}, u32[]{:S(2)}, u32[]{:S(2)}) collective-permute-start(bf16[104,875]{1,0:T(8,128)(2,1)S(1)} %slice.615), channel_id=1, source_target_pairs={{0,4},{2,6},{4,0},{6,2},{1,5},{3,7},{5,1},{7,3},{8,12},{10,14},{12... | collective-permute-start | bytes 546008 | tf_op jit(solution)/shard_map/ppermute | solution.py:33
  510.8 71.8 %collective-permute-start.45 = (bf16[4,875,256]{2,0,1:T(4,128)(2,1)}, bf16[4,875,256]{2,0,1:T(4,128)(2,1)S(1)}, u32[]{:S(2)}, u32[]{:S(2)}) collective-permute-start(bf16[4,875,256]{2,0,1:T(4,128)(2,1)} %copy.146), channel_id=1, source_target_pairs={{0,1},{1,0},{2,3},{3,2},{4,5},{5,4},{6,7},{7,6},{8,9},{9,8},{10,11... | collective-permute-start | bytes 5376008 | tf_op jit(solution)/shard_map/ppermute | solution.py:37
  532.9 24.6 %collective-permute-start.49 = (bf16[200,875]{1,0:T(8,128)(2,1)S(1)}, bf16[200,875]{1,0:T(8,128)(2,1)S(1)}, u32[]{:S(2)}, u32[]{:S(2)}) collective-permute-start(bf16[200,875]{1,0:T(8,128)(2,1)S(1)} %pad_maximum_fusion.16), channel_id=1, source_target_pairs={{0,4},{2,6},{4,0},{6,2},{1,5},{3,7},{5,1},{7,3},{8,12},{10,14},{12... | collective-permute-start | bytes 1050008 | tf_op jit(solution)/shard_map/ppermute | solution.py:33
  534.4 16.7 %collective-permute-start.53 = (bf16[200,875]{1,0:T(8,128)(2,1)S(1)}, bf16[200,875]{1,0:T(8,128)(2,1)S(1)}, u32[]{:S(2)}, u32[]{:S(2)}) collective-permute-start(bf16[200,875]{1,0:T(8,128)(2,1)S(1)} %pad_maximum_fusion.18), channel_id=1, source_target_pairs={{0,4},{2,6},{4,0},{6,2},{1,5},{3,7},{5,1},{7,3},{8,12},{10,14},{12... | collective-permute-start | bytes 1050008 | tf_op jit(solution)/shard_map/ppermute | solution.py:33
  536.4 15.1 %collective-permute-start.51 = (bf16[200,875]{1,0:T(8,128)(2,1)S(1)}, bf16[200,875]{1,0:T(8,128)(2,1)S(1)}, u32[]{:S(2)}, u32[]{:S(2)}) collective-permute-start(bf16[200,875]{1,0:T(8,128)(2,1)S(1)} %pad_maximum_fusion.17), channel_id=1, source_target_pairs={{0,2},{2,0},{4,6},{6,4},{1,3},{3,1},{5,7},{7,5},{8,10},{10,8},{12,... | collective-permute-start | bytes 1050008 | tf_op jit(solution)/shard_map/ppermute | solution.py:33
  537.5 14.0 %collective-permute-start.63 = (bf16[200,875]{1,0:T(8,128)(2,1)S(1)}, bf16[200,875]{1,0:T(8,128)(2,1)S(1)}, u32[]{:S(2)}, u32[]{:S(2)}) collective-permute-start(bf16[200,875]{1,0:T(8,128)(2,1)S(1)} %add_convert_fusion.4), channel_id=1, source_target_pairs={{0,8},{8,16},{16,24},{24,0},{1,9},{9,17},{17,25},{25,1},{2,10},{10... | collective-permute-start | bytes 1050008 | tf_op jit(solution)/shard_map/ppermute | solution.py:42
  (181 other events, 1878.2 us)
Sparse Core Ops, SparseCore 0:
  38.5 60.6 all-gather.4
  429.8 142.6 reduce-scatter.7
  574.9 133.4 reduce-scatter.5
